TPU v7x, 32 devices: a whole 2x2x4 slice. The times are simulated.
32 devices in a mesh: cb: 4 (over y, x), tp: 8 (over z, core).
Axes of the slice: x: 2, y: 2, z: 4, core: 2. Of those that a mesh axis runs over, the one named last changes fastest.
Arguments:
- hidden_in: bfloat16 [128, 4096], P('cb', 'tp'), may hold values from -6 to 6
- norm_gain: bfloat16 [4096], P('tp'), may hold values from 0.25 to 1.75
- w_qkv: bfloat16 [3, 4096, 4096], P(None, None, 'tp'), may hold values from -0.0625 to 0.0625
- w_out: bfloat16 [4096, 4096], P('tp'), may hold values from -0.09375 to 0.09375
- cache_keys: bfloat16 [128, 64, 4096], P(('cb', 'tp')), may hold values from -6 to 6
- cache_values: bfloat16 [128, 64, 4096], P(('cb', 'tp')), may hold values from -6 to 6
- lengths: int32 [128], P(('cb', 'tp')), may hold values from 2 to 64, as said below
- tokens: int32 [128, 8], P(None, 'cb'), may hold values from 0 to 2047
- w_in: bfloat16 [8, 4096, 1024], P('cb', 'tp'), may hold values from -0.09375 to 0.09375
- embed: bfloat16 [8, 2048, 1024], P('cb', None, 'tp'), may hold values from -6 to 6
- depth_gain: bfloat16 [8, 1024], P('cb'), may hold values from 0.25 to 1.75
- w_gate_up: bfloat16 [8, 2, 1024, 2816], P('cb', None, None, 'tp'), may hold values from -0.1875 to 0.1875
- w_down: bfloat16 [8, 2816, 1024], P('cb', 'tp'), may hold values from -0.109375 to 0.109375
Outputs:
- temporal_out: bfloat16 [128, 4096], P('cb', 'tp')
- depth_out: bfloat16 [8, 128, 1024], P('cb', None, 'tp')
Inputs may be any that keep to these rules, and one draw needn't show every extreme that they name: `lengths`: number of live cache slots of each stream-beam; some row has all 64.
All inputs are finite; a program needn't handle non-finite values.
Results may differ from a plain program's by a relative error of at most 0.009.
Values may be sent and summed in bfloat16 or wider, within the bound.
A program may use at most 64 MiB of HBM per device.

v0:
```python
import math

import jax
import jax.numpy as jnp
from jax import lax
from jax.sharding import PartitionSpec as P

D = 4096
HEADS = 32
HEAD_DIM = 128
DD = 1024
CARD = 2048
CACHE = 64


eps = 1e-05


def from_behind(value, axis, steps):
    count = lax.axis_size(axis)
    pairs = [(source, (source + steps) % count) for source in range(count)]
    return lax.ppermute(value, axis, pairs)


def per_device(
    hidden_in,
    norm_gain,
    w_qkv,
    w_out,
    cache_keys,
    cache_values,
    lengths,
    tokens,
    w_in,
    embed,
    depth_gain,
    w_gate_up,
    w_down,
):
    width_tp = lax.axis_size("tp")
    group_rows, feat_loc = hidden_in.shape
    hid32 = hidden_in.astype(jnp.float32)
    sum_sq = lax.psum(jnp.sum(hid32 * hid32, axis=1), "tp")
    normed = (hid32 * lax.rsqrt(sum_sq / D + eps)[:, None] * norm_gain.astype(jnp.float32)).astype(
        jnp.bfloat16
    )
    qkv = jnp.einsum(
        "rd,idf->rif",
        lax.all_gather(normed, "tp", axis=1, tiled=True),
        w_qkv,
        preferred_element_type=jnp.float32,
    ).astype(jnp.bfloat16)
    per_dev = group_rows // width_tp
    arrived = lax.all_to_all(
        qkv.reshape(width_tp, per_dev, 3, feat_loc), "tp", split_axis=0, concat_axis=3, tiled=True
    )
    arrived = arrived.reshape(per_dev, 3, D)
    scale = 1.0 / math.sqrt(HEAD_DIM)
    query_h = arrived[:, 0].reshape(per_dev, HEADS, HEAD_DIM)
    key_new = arrived[:, 1].reshape(per_dev, HEADS, HEAD_DIM)
    value_new = arrived[:, 2].reshape(per_dev, HEADS, HEAD_DIM)
    keys_h = cache_keys.reshape(per_dev, CACHE, HEADS, HEAD_DIM)
    values_h = cache_values.reshape(per_dev, CACHE, HEADS, HEAD_DIM)
    scores = (
        jnp.einsum("rhe,rphe->rhp", query_h, keys_h, preferred_element_type=jnp.float32) * scale
    )
    live = lax.broadcasted_iota(jnp.int32, (1, 1, CACHE), 2) < lengths[:, None, None]
    scores = jnp.where(live, scores, -1e30)
    fresh = jnp.sum(query_h.astype(jnp.float32) * key_new.astype(jnp.float32), axis=-1) * scale
    top = jnp.maximum(jnp.max(scores, axis=-1), fresh)
    weights = jnp.exp(scores - top[..., None])
    weight_new = jnp.exp(fresh - top)
    total = jnp.sum(weights, axis=-1) + weight_new
    probs = (weights / total[..., None]).astype(jnp.bfloat16)
    prob_new = (weight_new / total).astype(jnp.bfloat16)
    mixed = jnp.einsum("rhp,rphe->rhe", probs, values_h, preferred_element_type=jnp.float32)
    mixed = mixed + prob_new.astype(jnp.float32)[..., None] * value_new.astype(jnp.float32)
    attended = mixed.reshape(per_dev, width_tp, feat_loc).astype(jnp.bfloat16)
    returned = lax.all_to_all(attended, "tp", split_axis=1, concat_axis=0, tiled=True).reshape(
        group_rows, feat_loc
    )
    partial_value = jnp.dot(returned, w_out, preferred_element_type=jnp.float32)
    attn_sum = lax.psum_scatter(partial_value, "tp", scatter_dimension=1, tiled=True)
    temporal_out = (hid32 + attn_sum).astype(jnp.bfloat16)
    frame = lax.all_gather(temporal_out, "cb", axis=0, tiled=True)
    steps_here = w_in.shape[0]
    depth_loc = embed.shape[2]
    column_start = lax.axis_index("tp") * depth_loc
    codes = lax.broadcasted_iota(jnp.int32, (1, CARD), 1)
    embedded = []
    for local in range(steps_here):
        one_hot = (tokens[:, local][:, None] == codes).astype(jnp.bfloat16)
        embedded.append(
            jnp.dot(one_hot, embed[local], preferred_element_type=jnp.float32).astype(jnp.bfloat16)
        )
    carried = from_behind(embedded[steps_here - 1], "cb", 1)
    previous = [carried] + embedded[: steps_here - 1]
    results = []
    for local in range(steps_here):
        term = jnp.dot(frame, w_in[local], preferred_element_type=jnp.float32)
        gain_all = depth_gain[local].astype(jnp.float32)
        x_loc = lax.psum_scatter(term, "tp", scatter_dimension=1, tiled=True) + previous[
            local
        ].astype(jnp.float32)
        sum_d = lax.psum(jnp.sum(x_loc * x_loc, axis=1), "tp")
        gain_loc = lax.dynamic_slice_in_dim(gain_all, column_start, depth_loc, 0)
        xn_loc = (x_loc * lax.rsqrt(sum_d / DD + eps)[:, None] * gain_loc).astype(jnp.bfloat16)
        weights_step = w_gate_up[local]
        gate_up = jnp.einsum(
            "rd,idf->irf",
            lax.all_gather(xn_loc, "tp", axis=1, tiled=True),
            weights_step,
            preferred_element_type=jnp.float32,
        )
        act = (jax.nn.silu(gate_up[0]) * gate_up[1]).astype(jnp.bfloat16)
        down_term = jnp.dot(act, w_down[local], preferred_element_type=jnp.float32)
        down_sum = lax.psum_scatter(down_term, "tp", scatter_dimension=1, tiled=True)
        results.append((x_loc + down_sum).astype(jnp.bfloat16))
    return (temporal_out, jnp.stack(results))


def solution(mesh):
    in_specs = (
        P("cb", "tp"),
        P("tp"),
        P(None, None, "tp"),
        P("tp", None),
        P(("cb", "tp"), None, None),
        P(("cb", "tp"), None, None),
        P(("cb", "tp")),
        P(None, "cb"),
        P("cb", "tp", None),
        P("cb", None, "tp"),
        P("cb", None),
        P("cb", None, None, "tp"),
        P("cb", "tp", None),
    )
    out_specs = (P("cb", "tp"), P("cb", None, "tp"))
    return jax.shard_map(
        per_device, mesh=mesh, in_specs=in_specs, out_specs=out_specs, check_vma=False
    )
```

profile of v0, /device:TPU:0, one launch (start us, length us, event | category | flops | bytes accessed | tf_op | source)
XLA Modules:
  0.0 276.5 jit_solution(7756908933129002592)
XLA Ops:
  7.2 0.8 convert_element_type.108
  8.0 0.9 fusion.47
  8.9 18.1 %psum.21 = f32[32]{0:T(128)S(1)} all-reduce(f32[32]{0:T(128)S(1)} %fusion.47), channel_id=1, replica_groups=mesh['cb'=4,'tp'=8] {'tp'}, use_global_device_ids=true, to_apply=%region_1.0 | all-reduce | flops 32 | bytes 256 | tf_op jit(solution)/shard_map/psum | solution.py:43
  27.0 0.8 fusion.49
  27.8 14.2 %all_gather.12 = bf16[32,4096]{1,0:T(8,128)(2,1)S(1)} all-gather(bf16[32,512]{1,0:T(8,128)(2,1)S(1)} %fusion.49), channel_id=1, replica_groups=mesh['cb'=4,'tp'=8] {'tp'}, dimensions={1}, use_global_device_ids=true | all-gather | bytes 294912 | tf_op jit(solution)/shard_map/all_gather | solution.py:49
  42.0 6.7 %convolution_convert_fusion = bf16[32,3,512]{2,0,1:T(8,128)(2,1)S(1)} fusion(bf16[3,4096,512]{2,1,0:T(8,128)(2,1)} %param.15, bf16[32,4096]{1,0:T(8,128)(2,1)S(1)} %all_gather.12), kind=kOutput, calls=%fused_computation.14 | convolution fusion | flops 402702336 | bytes 12943360 | tf_op jit(solution)/shard_map/rd,idf->rif/dot_general | solution.py:47
  48.8 0.7 copy.25
  49.4 3.4 %all-to-all-start = ((bf16[8,4,3,512]{3,1,2,0:T(4,128)(2,1)}), bf16[8,4,3,512]{3,1,2,0:T(4,128)(2,1)S(1)}, u32[]{:S(2)}, u32[]{:S(2)}) async-start(bf16[8,4,3,512]{3,1,2,0:T(4,128)(2,1)} %copy.25), calls=%async_computation | async-start | bytes 196608 | tf_op jit(solution)/shard_map/all_to_all | solution.py:54
  52.8 0.0 reduce-scatter.6.cloned.1.call-start
  52.9 0.1 iota_compare_fusion.4
  52.9 6.1 %all-to-all-done = bf16[8,4,3,512]{3,1,2,0:T(4,128)(2,1)S(1)} async-done(((bf16[8,4,3,512]{3,1,2,0:T(4,128)(2,1)}), bf16[8,4,3,512]{3,1,2,0:T(4,128)(2,1)S(1)}, u32[]{:S(2)}, u32[]{:S(2)}) %all-to-all-start) | async-done | bytes 98336 | tf_op jit(solution)/shard_map/all_to_all | solution.py:54
  59.2 0.1 reshape.99
  59.2 0.1 fusion.53
  59.3 2.8 %fusion.3 = f32[4,32,1,64]{3,2,1,0:T(1,128)S(1)} fusion(bf16[4,32,128,1]{2,3,1,0:T(2,128)(2,1)S(1)} %reshape.99, bf16[4,64,4096]{2,1,0:T(8,128)(2,1)} %param.17), kind=kOutput, calls=%fused_computation.3 | convolution fusion | flops 2097152 | bytes 2162688 | tf_op jit(solution)/shard_map/rhe,rphe->rhp/dot_general | solution.py:65
  62.1 0.1 fusion.55
  62.2 0.2 fusion.56
  62.4 0.1 fusion.59
  62.6 0.6 fusion
  63.2 0.1 fusion.52
  63.4 8.1 %all_to_all.30 = bf16[4,8,512]{2,0,1:T(4,128)(2,1)S(1)} all-to-all(bf16[4,8,512]{2,0,1:T(4,128)(2,1)S(1)} %copy.27), channel_id=1, replica_groups=mesh['cb'=4,'tp'=8] {'tp'}, dimensions={1} | all-to-all | bytes 65536 | tf_op jit(solution)/shard_map/all_to_all | solution.py:79
  71.5 3.8 %fusion.67 = f32[32,4096]{1,0:T(8,128)} fusion(bf16[32,512]{1,0:T(8,128)(2,1)S(1)} %reshape.88, bf16[512,4096]{1,0:T(8,128)(2,1)} %param.16), kind=kOutput, calls=%fused_computation.98 | convolution fusion | flops 134217728 | bytes 4751360 | tf_op jit(solution)/shard_map/dot_general | solution.py:82
  75.4 0.0 reduce-scatter.12.cloned.1.call-start
  75.4 29.4 %reduce-scatter.6.cloned.1.call-done = f32[32,512]{1,0:T(8,128)} async-done(((f32[32,4096]{1,0:T(8,128)}), f32[32,512]{1,0:T(8,128)}) %reduce-scatter.6.cloned.1.call-update) | async-done | bytes 65552 | tf_op jit(solution)/shard_map/reduce_scatter | solution.py:83
  104.8 0.8 fusion.50
  105.6 8.4 %all_gather.13 = bf16[128,512]{1,0:T(8,128)(2,1)S(1)} all-gather(bf16[32,512]{1,0:T(8,128)(2,1)S(1)} %fusion.50), channel_id=1, replica_groups=mesh['cb'=4,'tp'=8] {'cb'}, dimensions={0}, use_global_device_ids=true | all-gather | bytes 163840 | tf_op jit(solution)/shard_map/all_gather | solution.py:85
  114.0 2.4 fusion.20
  116.5 0.0 reduce-scatter.8.cloned.1.call-start
  116.5 2.4 fusion.22
  119.0 0.4 convolution_convert_fusion.2
  119.4 1.5 collective-permute-start
  120.9 23.9 %reduce-scatter.12.cloned.1.call-done = f32[128,128]{1,0:T(8,128)} async-done(((f32[128,1024]{1,0:T(8,128)}), f32[128,128]{1,0:T(8,128)}) %reduce-scatter.12.cloned.1.call-update) | async-done | bytes 65552 | tf_op jit(solution)/shard_map/reduce_scatter | solution.py:102
  144.8 1.3 multiply_reduce_fusion
  146.1 30.1 %reduce-scatter.8.cloned.1.call-done = f32[128,128]{1,0:T(8,128)} async-done(((f32[128,1024]{1,0:T(8,128)}), f32[128,128]{1,0:T(8,128)}) %reduce-scatter.8.cloned.1.call-update) | async-done | bytes 65552 | tf_op jit(solution)/shard_map/reduce_scatter | solution.py:102
  176.3 0.9 multiply_reduce_fusion.1
  177.2 13.7 %all-reduce = (f32[128]{0:T(128)S(1)}, f32[128]{0:T(128)S(1)}) all-reduce(f32[128]{0:T(128)S(1)} %get-tuple-element.14, f32[128]{0:T(128)S(1)} %multiply_reduce_fusion.1), channel_id=1, replica_groups=mesh['cb'=4,'tp'=8] {'tp'}, use_global_device_ids=true, to_apply=%region_12.13 | all-reduce | flops 256 | bytes 2048 | tf_op jit(solution)/shard_map/psum | solution.py:105
  191.0 0.1 multiply_convert_fusion
  191.1 13.2 %all_gather.15 = bf16[128,1024]{1,0:T(8,128)(2,1)S(1)} all-gather(bf16[128,128]{1,0:T(8,128)(2,1)S(1)} %multiply_convert_fusion), channel_id=1, replica_groups=mesh['cb'=4,'tp'=8] {'tp'}, dimensions={1}, use_global_device_ids=true | all-gather | bytes 294912 | tf_op jit(solution)/shard_map/all_gather | solution.py:111
  204.3 1.9 fusion.15
  206.2 1.1 fusion.26
  207.5 0.1 multiply_convert_fusion.1
  207.6 13.3 %all_gather.14 = bf16[128,1024]{1,0:T(8,128)(2,1)S(1)} all-gather(bf16[128,128]{1,0:T(8,128)(2,1)S(1)} %multiply_convert_fusion.1), channel_id=1, replica_groups=mesh['cb'=4,'tp'=8] {'tp'}, dimensions={1}, use_global_device_ids=true | all-gather | bytes 294912 | tf_op jit(solution)/shard_map/all_gather | solution.py:111
  220.9 1.9 fusion.12
  222.8 1.2 fusion.28
  224.0 13.1 %reduce-scatter.14.cloned.1.call-done = f32[128,128]{1,0:T(8,128)} async-done(((f32[128,1024]{1,0:T(8,128)}), f32[128,128]{1,0:T(8,128)}) %reduce-scatter.14.cloned.1.call-update) | async-done | bytes 65552 | tf_op jit(solution)/shard_map/reduce_scatter | solution.py:117
  237.1 0.8 fusion.58
  238.0 30.5 %reduce-scatter.10.cloned.1.call-done = f32[128,128]{1,0:T(8,128)} async-done(((f32[128,1024]{1,0:T(8,128)}), f32[128,128]{1,0:T(8,128)}) %reduce-scatter.10.cloned.1.call-update) | async-done | bytes 65552 | tf_op jit(solution)/shard_map/reduce_scatter | solution.py:117
  268.5 0.9 fusion.57
  269.4 0.6 pad_maximum_fusion
  (44 shorter events, 0.5 us)
Async XLA Ops:
  7.2 55.4 %copy-start = (bf16[4,64,4096]{2,1,0:T(8,128)(2,1)S(1)}, bf16[4,64,4096]{2,1,0:T(8,128)(2,1)}, u32[]{:S(2)}) copy-start(bf16[4,64,4096]{2,1,0:T(8,128)(2,1)} %param.18) | copy-start | bytes 6291460
  42.0 10.9 %copy-start.9 = (s32[4]{0:T(128)S(1)}, s32[4]{0:T(128)}, u32[]{:S(2)}) copy-start(s32[4]{0:T(128)} %param.19) | copy-start | bytes 52
  49.4 9.6 %all-to-all-start = ((bf16[8,4,3,512]{3,1,2,0:T(4,128)(2,1)}), bf16[8,4,3,512]{3,1,2,0:T(4,128)(2,1)S(1)}, u32[]{:S(2)}, u32[]{:S(2)}) async-start(bf16[8,4,3,512]{3,1,2,0:T(4,128)(2,1)} %copy.25), calls=%async_computation | async-start | bytes 196608 | tf_op jit(solution)/shard_map/all_to_all | solution.py:54
  52.8 52.0 %reduce-scatter.6.cloned.1.call-start = ((), (), s32[]{:S(2)}) async-start(), calls=%async_computation.7 | async-start | bytes 589824 | tf_op jit(solution)/shard_map/reduce_scatter | solution.py:83
  71.5 33.3 %copy-start.2 = (bf16[32,512]{1,0:T(8,128)(2,1)S(1)}, bf16[32,512]{1,0:T(8,128)(2,1)}, u32[]{:S(2)}) copy-start(bf16[32,512]{1,0:T(8,128)(2,1)} %param.13) | copy-start | bytes 98308
  75.4 69.5 %reduce-scatter.12.cloned.1.call-start = ((), (), s32[]{:S(2)}) async-start(), calls=%async_computation.10 | async-start | bytes 589824 | tf_op jit(solution)/shard_map/reduce_scatter | solution.py:102
  105.6 13.3 %copy-start.3 = (bf16[32,512]{1,0:T(8,128)(2,1)}, bf16[32,512]{1,0:T(8,128)(2,1)S(1)}, u32[]{:S(2)}) copy-start(bf16[32,512]{1,0:T(8,128)(2,1)S(1)} %fusion.50) | copy-start | bytes 98308
  114.0 4.9 %copy-start.5 = (s32[128,2]{0,1:T(2,128)S(1)}, s32[128,2]{0,1:T(2,128)}, u32[]{:S(2)}) copy-start(s32[128,2]{0,1:T(2,128)} %param.20) | copy-start | bytes 3076
  114.0 5.0 %copy-start.8 = (bf16[2,2048,128]{2,1,0:T(8,128)(2,1)S(1)}, bf16[2,2048,128]{2,1,0:T(8,128)(2,1)}, u32[]{:S(2)}) copy-start(bf16[2,2048,128]{2,1,0:T(8,128)(2,1)} %param.22) | copy-start | bytes 3145732
  116.5 4.4 %copy-start.4 = (bf16[2,1024]{1,0:T(2,128)(2,1)S(1)}, bf16[2,1024]{1,0:T(2,128)(2,1)}, u32[]{:S(2)}) copy-start(bf16[2,1024]{1,0:T(2,128)(2,1)} %param.23) | copy-start | bytes 12292
  116.5 59.8 %reduce-scatter.8.cloned.1.call-start = ((), (), s32[]{:S(2)}) async-start(), calls=%async_computation.8 | async-start | bytes 589824 | tf_op jit(solution)/shard_map/reduce_scatter | solution.py:102
  118.9 118.2 %reduce-scatter.14.cloned.1.call-start = ((), (), s32[]{:S(2)}) async-start(), calls=%async_computation.11 | async-start | bytes 589824 | tf_op jit(solution)/shard_map/reduce_scatter | solution.py:117
  119.4 26.8 %collective-permute-start = (bf16[128,128]{1,0:T(8,128)(2,1)S(1)}, bf16[128,128]{1,0:T(8,128)(2,1)S(1)}, u32[]{:S(2)}, u32[]{:S(2)}) collective-permute-start(bf16[128,128]{1,0:T(8,128)(2,1)S(1)} %convolution_convert_fusion.2), channel_id=1, source_target_pairs={{0,8},{8,16},{16,24},{24,0},{1,9},{9,17},{17,25},{25,1},{2,10},{10... | collective-permute-start | bytes 98312 | tf_op jit(solution)/shard_map/ppermute | solution.py:22
  191.0 15.3 %copy-start.6 = (bf16[2,352,1024]{2,1,0:T(8,128)(2,1)S(1)}, bf16[2,352,1024]{2,1,0:T(8,128)(2,1)}, u32[]{:S(2)}) copy-start(bf16[2,352,1024]{2,1,0:T(8,128)(2,1)} %param.25) | copy-start | bytes 4325380
  204.3 3.2 %copy-start.1 = (f32[128,128]{1,0:T(8,128)S(1)}, f32[128,128]{1,0:T(8,128)}, u32[]{:S(2)}) copy-start(f32[128,128]{1,0:T(8,128)} %reduce-scatter.8.cloned.1.call-done) | copy-start | bytes 196612
  207.4 61.1 %reduce-scatter.10.cloned.1.call-start = ((), (), s32[]{:S(2)}) async-start(), calls=%async_computation.9 | async-start | bytes 589824 | tf_op jit(solution)/shard_map/reduce_scatter | solution.py:117
  207.5 15.3 %copy-start.7 = (bf16[2,352,1024]{2,1,0:T(8,128)(2,1)S(1)}, bf16[2,352,1024]{2,1,0:T(8,128)(2,1)}, u32[]{:S(2)}) copy-start(bf16[2,352,1024]{2,1,0:T(8,128)(2,1)} %param.25) | copy-start | bytes 4325380
Sparse Core Ops, SparseCore 0:
  75.5 29.2 reduce-scatter.5
  116.6 28.1 reduce-scatter.11
  147.1 29.1 reduce-scatter.7
  207.5 29.5 reduce-scatter.13
  239.2 29.2 reduce-scatter.9
where the time goes:
time: 277 us
  waiting for transfers between devices  133 us (48%)
  blocking collectives  89.1 us (32%)
  matrix products  26.5 us (10%)
  between operations  14.1 us (5%)
  other arithmetic  7.6 us (3%)
  starting transfers between devices  5.08 us (2%)
    reduce_scatter x2, waiting for transfers between devices, per_device(): lax.psum_scatter(term, 'tp', scatter_dimension=1, tiled=True)  54 us
    reduce_scatter x2, waiting for transfers between devices, per_device(): lax.psum_scatter(down_term, 'tp', scatter_dimension=1, tiled=True)  43.7 us
    reduce_scatter x1, waiting for transfers between devices, per_device(): lax.psum_scatter(partial_value, 'tp', scatter_dimension=1, tiled=True)  29.4 us
    all_gather x2, blocking collectives, per_device(): lax.all_gather(xn_loc, 'tp', axis=1, tiled=True)  26.5 us
    psum x1, blocking collectives, per_device(): sum_sq = lax.psum(jnp.sum(hid32 * hid32, axis=1), 'tp')  18.1 us
    all_gather x1, blocking collectives, per_device(): lax.all_gather(normed, 'tp', axis=1, tiled=True)  14.2 us
    psum x1, blocking collectives, per_device(): sum_d = lax.psum(jnp.sum(x_loc * x_loc, axis=1), 'tp')  13.7 us
    all_gather x1, blocking collectives, per_device(): frame = lax.all_gather(temporal_out, 'cb', axis=0, tiled=True)  8.42 us
  transfers between devices with their start and end apart: 7, of which 6 were waited for; matrix products, arithmetic and copies ran while one was open for 3% of the time, Pallas kernels for 0%

commit v1 on v0

--- a/solution.py
+++ b/solution.py
@@ -1,8 +1,11 @@
+import functools
 import math
 
 import jax
 import jax.numpy as jnp
 from jax import lax
+from jax.experimental import pallas as pl
+from jax.experimental.pallas import tpu as pltpu
 from jax.sharding import PartitionSpec as P
 
 D = 4096
@@ -119,6 +122,415 @@
     return (temporal_out, jnp.stack(results))
 
 
+MESH = pl.DeviceIdType.MESH
+NORM, GAIN, CARRY, QKV, BACK, OUT, FRAME, XSUM, XN, DOWN = 0, 1, 2, 3, 4, 5, 6, 7, 9, 11
+PHASES = 13
+
+
+def frame_kernel(
+    ntp,
+    ncb,
+    hid,
+    gain,
+    lengths,
+    tokens,
+    depth_gain,
+    w_qkv,
+    w_out,
+    keys,
+    values,
+    w_in,
+    embed,
+    w_gu,
+    w_down,
+    out_t,
+    out_d,
+    vq,
+    vo,
+    vk,
+    vv,
+    vi,
+    ve,
+    vg,
+    vd,
+    hid_all,
+    gain_all,
+    normed,
+    qkv_send,
+    qkv_recv,
+    att_send,
+    att_recv,
+    returned,
+    o_send,
+    o_recv,
+    frame,
+    emb,
+    carried,
+    part,
+    x_send,
+    x_recv,
+    x_own,
+    xn_all,
+    d_send,
+    d_recv,
+    wsem,
+    ssem,
+    rsem,
+):
+    f32, bf16 = jnp.float32, jnp.bfloat16
+    me = lax.axis_index("tp")
+    grp = lax.axis_index("cb")
+    rows, feat = hid.shape
+    per_dev = rows // ntp
+    heads = feat // HEAD_DIM
+    blk = per_dev * heads
+    steps = w_in.shape[0]
+    drows = frame.shape[0] * rows // ntp
+    dfeat = DD // ntp
+    order = sorted(range(1, ntp), key=lambda i: abs(i - ntp // 2))
+
+    weights = {}
+
+    def load(name, source, target, index):
+        copy = pltpu.make_async_copy(source, target, wsem.at[index])
+        copy.start()
+        weights[name] = copy
+
+    for i in range(3):
+        load(("q", i), w_qkv.at[i], vq.at[i], i)
+    load("e", embed, ve, 3)
+
+    sent = []
+
+    def put(source, target, phase, i, axis, device):
+        copy = pltpu.make_async_remote_copy(
+            src_ref=source,
+            dst_ref=target,
+            send_sem=ssem.at[phase, i],
+            recv_sem=rsem.at[phase, i],
+            device_id={axis: device},
+            device_id_type=MESH,
+        )
+        copy.start()
+        sent.append(copy)
+        return copy
+
+    def tp_at(i):
+        return lax.rem(me + i, ntp)
+
+    def cb_at(i):
+        return lax.rem(grp + i, ncb)
+
+    barrier = pltpu.get_barrier_semaphore()
+    for i in range(1, ntp):
+        pl.semaphore_signal(barrier, inc=1, device_id={"tp": tp_at(i)}, device_id_type=MESH)
+    for i in range(1, ncb):
+        pl.semaphore_signal(barrier, inc=1, device_id={"cb": cb_at(i)}, device_id_type=MESH)
+
+    gain32 = gain[...].astype(f32)
+    gain_rows = [gain32[:, h * HEAD_DIM : (h + 1) * HEAD_DIM] for h in range(heads)]
+    gain_rows.append(jnp.zeros((16 - heads, HEAD_DIM), f32))
+    gain_all[me] = jnp.concatenate(gain_rows, axis=0).astype(bf16)
+    hid_all[me] = hid[...]
+    pl.semaphore_wait(barrier, ntp - 1 + ncb - 1)
+
+    arriving = []
+    for i in order:
+        arriving.append(put(hid_all.at[me], hid_all.at[me], NORM, i, "tp", tp_at(i)))
+        arriving.append(put(gain_all.at[me], gain_all.at[me], GAIN, i, "tp", tp_at(i)))
+
+    weights["e"].wait()
+    codes = lax.broadcasted_iota(jnp.int32, (tokens.shape[0], CARD), 1)
+    for local in range(steps):
+        one_hot = (tokens[:, local : local + 1] == codes).astype(f32).astype(bf16)
+        emb[local] = jnp.dot(one_hot, ve[local], preferred_element_type=f32).astype(bf16)
+    carry = put(emb.at[steps - 1], carried, CARRY, 1, "cb", cb_at(1))
+
+    for copy in arriving:
+        copy.wait_recv()
+    load("k", keys, vk, 4)
+    load("v", values, vv, 5)
+    load("o", w_out, vo, 6)
+    load("i", w_in, vi, 7)
+    load("g", w_gu, vg, 8)
+    load("d", w_down, vd, 9)
+
+    total = jnp.zeros((rows, 1), f32)
+    for s in range(ntp):
+        piece = hid_all[s].astype(f32)
+        total = total + jnp.sum(piece * piece, axis=1, keepdims=True)
+    inv = lax.rsqrt(total / D + eps)
+    for s in range(ntp):
+        piece = hid_all[s].astype(f32)
+        gains = gain_all[s].astype(f32)
+        for h in range(heads):
+            cols = slice(h * HEAD_DIM, (h + 1) * HEAD_DIM)
+            at = s * feat + h * HEAD_DIM
+            normed[:, at : at + HEAD_DIM] = (
+                piece[:, cols] * inv * gains[h : h + 1, :]
+            ).astype(bf16)
+
+    size = rows * heads
+    place = lax.broadcasted_iota(jnp.int32, (size, size), 0)
+    column = lax.broadcasted_iota(jnp.int32, (size, size), 1)
+    source = ((place // per_dev) % heads) * rows + (place // blk) * per_dev + place % per_dev
+    perm = (column == source).astype(f32).astype(bf16)
+    for i in range(3):
+        weights["q", i].wait()
+        full = jnp.dot(normed[...], vq[i], preferred_element_type=f32).astype(bf16)
+        stacked = jnp.concatenate(
+            [full[:, h * HEAD_DIM : (h + 1) * HEAD_DIM] for h in range(heads)], axis=0
+        )
+        moved = jnp.dot(perm, stacked, preferred_element_type=f32).astype(bf16)
+        qkv_send[:, i * blk : (i + 1) * blk, :] = moved.reshape(ntp, blk, HEAD_DIM)
+    arriving = [
+        put(qkv_send.at[tp_at(i)], qkv_recv.at[me], QKV, i, "tp", tp_at(i)) for i in order
+    ]
+    qkv_recv[me] = qkv_send[me]
+    weights["k"].wait()
+    weights["v"].wait()
+    for copy in arriving:
+        copy.wait_recv()
+
+    scale = 1.0 / math.sqrt(HEAD_DIM)
+    slots = per_dev * CACHE
+    row = lax.broadcasted_iota(jnp.int32, (blk, slots), 0)
+    col = lax.broadcasted_iota(jnp.int32, (blk, slots), 1)
+    count = jnp.zeros((blk, slots), jnp.int32)
+    for r in range(per_dev):
+        count = jnp.where(col // CACHE == r, lengths[r], count)
+    live = (row % per_dev == col // CACHE) & (col % CACHE < count)
+    head_of = lax.broadcasted_iota(jnp.int32, (blk, HEAD_DIM), 0) // per_dev
+    for s in range(ntp):
+        query = qkv_recv[s, 0:blk, :].astype(f32)
+        key_new = qkv_recv[s, blk : 2 * blk, :].astype(f32)
+        value_new = qkv_recv[s, 2 * blk : 3 * blk, :].astype(f32)
+        spread = jnp.concatenate(
+            [jnp.where(head_of == h, query, 0.0) for h in range(heads)], axis=1
+        ).astype(bf16)
+        cols = slice(s * feat, (s + 1) * feat)
+        old_keys = vk[:, :, cols].reshape(slots, feat)
+        scores = (
+            lax.dot_general(
+                spread, old_keys, (((1,), (1,)), ((), ())), preferred_element_type=f32
+            )
+            * scale
+        )
+        scores = jnp.where(live, scores, -1e30)
+        fresh = jnp.sum(query * key_new, axis=1, keepdims=True) * scale
+        top = jnp.maximum(jnp.max(scores, axis=1, keepdims=True), fresh)
+        weight = jnp.exp(scores - top)
+        weight_new = jnp.exp(fresh - top)
+        norm = jnp.sum(weight, axis=1, keepdims=True) + weight_new
+        probs = (weight / norm).astype(bf16)
+        prob_new = (weight_new / norm).astype(bf16).astype(f32)
+        old_values = vv[:, :, cols].reshape(slots, feat)
+        wide = jnp.dot(probs, old_values, preferred_element_type=f32)
+        mixed = prob_new * value_new
+        for h in range(heads):
+            mixed = mixed + jnp.where(
+                head_of == h, wide[:, h * HEAD_DIM : (h + 1) * HEAD_DIM], 0.0
+            )
+        att_send[s] = mixed.astype(bf16)
+    arriving = [
+        put(att_send.at[tp_at(i)], att_recv.at[me], BACK, i, "tp", tp_at(i)) for i in order
+    ]
+    att_recv[me] = att_send[me]
+    for copy in arriving:
+        copy.wait_recv()
+    gathered = att_recv[...].reshape(ntp * blk, HEAD_DIM)
+    place = lax.broadcasted_iota(jnp.int32, (rows, ntp * blk), 0)
+    column = lax.broadcasted_iota(jnp.int32, (rows, ntp * blk), 1)
+    for h in range(heads):
+        source = (place // per_dev) * blk + h * per_dev + place % per_dev
+        pick = (column == source).astype(f32).astype(bf16)
+        returned[:, h * HEAD_DIM : (h + 1) * HEAD_DIM] = jnp.dot(
+            pick, gathered, preferred_element_type=f32
+        ).astype(bf16)
+
+    weights["o"].wait()
+    arriving = []
+    for i in order + [0]:
+        cols = pl.ds(pl.multiple_of(tp_at(i) * feat, feat), feat)
+        term = jnp.dot(returned[...], vo[:, cols], preferred_element_type=f32)
+        if i == 0:
+            attn = term
+        else:
+            o_send[i] = term.astype(bf16)
+            arriving.append(put(o_send.at[i], o_recv.at[i], OUT, i, "tp", tp_at(i)))
+    for copy in arriving:
+        copy.wait_recv()
+    for i in range(1, ntp):
+        attn = attn + o_recv[i].astype(f32)
+    temporal = (hid[...].astype(f32) + attn).astype(bf16)
+    out_t[...] = temporal
+    frame[grp] = temporal
+
+    arriving = [
+        put(frame.at[grp], frame.at[grp], FRAME, i, "cb", cb_at(i)) for i in range(1, ncb)
+    ]
+    weights["i"].wait()
+    carry.wait_recv()
+    for copy in arriving:
+        copy.wait_recv()
+    lhs = frame[...].reshape(ncb * rows, feat)
+
+    arriving = []
+    own_cols = pl.ds(pl.multiple_of(me * dfeat, dfeat), dfeat)
+    for local in range(steps):
+        part[...] = jnp.dot(lhs, vi[local], preferred_element_type=f32)
+        before = carried[...] if local == 0 else emb[local - 1]
+        part[:, own_cols] = part[:, own_cols] + before.astype(f32)
+        x_send[local] = part[...].astype(bf16).reshape(ntp, drows, DD)
+        arriving.append(
+            [
+                put(
+                    x_send.at[local, tp_at(i)], x_recv.at[local, i], XSUM + local, i, "tp", tp_at(i)
+                )
+                for i in order
+            ]
+        )
+        own_rows = pl.ds(pl.multiple_of(me * drows, drows), drows)
+        x_own[local] = part[own_rows, :]
+    gathers = []
+    for local in range(steps):
+        for copy in arriving[local]:
+            copy.wait_recv()
+        x = x_own[local]
+        for i in range(1, ntp):
+            x = x + x_recv[local, i].astype(f32)
+        x_own[local] = x
+        inv = lax.rsqrt(jnp.sum(x * x, axis=1, keepdims=True) / DD + eps)
+        gains = depth_gain[local : local + 1, :].astype(f32)
+        xn_all[local, me] = (x * inv * gains).astype(bf16)
+        gathers.append(
+            [
+                put(xn_all.at[local, me], xn_all.at[local, me], XN + local, i, "tp", tp_at(i))
+                for i in order
+            ]
+        )
+
+    weights["g"].wait()
+    weights["d"].wait()
+    arriving = []
+    for local in range(steps):
+        for copy in gathers[local]:
+            copy.wait_recv()
+        lhs = xn_all[local].reshape(ntp * drows, DD)
+        gate = jnp.dot(lhs, vg[local, 0], preferred_element_type=f32)
+        upper = jnp.dot(lhs, vg[local, 1], preferred_element_type=f32)
+        act = (jax.nn.silu(gate) * upper).astype(bf16)
+        part[...] = jnp.dot(act, vd[local], preferred_element_type=f32)
+        own_rows = pl.ds(pl.multiple_of(me * drows, drows), drows)
+        part[own_rows, :] = part[own_rows, :] + x_own[local]
+        copies = []
+        for i in order:
+            cols = pl.ds(pl.multiple_of(tp_at(i) * dfeat, dfeat), dfeat)
+            d_send[local, i] = part[:, cols].astype(bf16)
+            copies.append(
+                put(d_send.at[local, i], d_recv.at[local, i], DOWN + local, i, "tp", tp_at(i))
+            )
+        arriving.append(copies)
+        out_d[local] = part[:, own_cols]
+    for local in range(steps):
+        for copy in arriving[local]:
+            copy.wait_recv()
+        y = out_d[local]
+        for i in range(1, ntp):
+            y = y + d_recv[local, i].astype(f32)
+        out_d[local] = y
+    for copy in sent:
+        copy.wait_send()
+
+
+def fits(mesh, hidden_in, w_in):
+    ntp, ncb = mesh.shape["tp"], mesh.shape["cb"]
+    rows, feat = hidden_in.shape[0] // ncb, hidden_in.shape[1] // ntp
+    steps = w_in.shape[0] // ncb
+    return (
+        steps == 2
+        and feat % HEAD_DIM == 0
+        and feat // HEAD_DIM <= 16
+        and rows % ntp == 0
+        and (rows // ntp * (feat // HEAD_DIM)) % 16 == 0
+        and (rows * ncb) % (16 * ntp) == 0
+        and (DD // ntp) % 128 == 0
+    )
+
+
+def fused(
+    hidden_in,
+    norm_gain,
+    w_qkv,
+    w_out,
+    cache_keys,
+    cache_values,
+    lengths,
+    tokens,
+    w_in,
+    embed,
+    depth_gain,
+    w_gate_up,
+    w_down,
+):
+    ntp, ncb = lax.axis_size("tp"), lax.axis_size("cb")
+    f32, bf16 = jnp.float32, jnp.bfloat16
+    rows, feat = hidden_in.shape
+    blk = rows // ntp * (feat // HEAD_DIM)
+    steps = w_in.shape[0]
+    total_rows = rows * ncb
+    drows, dfeat = total_rows // ntp, DD // ntp
+    vmem = pl.BlockSpec(memory_space=pltpu.VMEM)
+    hbm = pl.BlockSpec(memory_space=pl.ANY)
+    big = [w_qkv, w_out, cache_keys, cache_values, w_in, embed, w_gate_up, w_down]
+    scratch = [pltpu.VMEM(a.shape, a.dtype) for a in big] + [
+        pltpu.VMEM((ntp, rows, feat), bf16),
+        pltpu.VMEM((ntp, 16, HEAD_DIM), bf16),
+        pltpu.VMEM((rows, D), bf16),
+        pltpu.VMEM((ntp, 3 * blk, HEAD_DIM), bf16),
+        pltpu.VMEM((ntp, 3 * blk, HEAD_DIM), bf16),
+        pltpu.VMEM((ntp, blk, HEAD_DIM), bf16),
+        pltpu.VMEM((ntp, blk, HEAD_DIM), bf16),
+        pltpu.VMEM((rows, feat), bf16),
+        pltpu.VMEM((ntp, rows, feat), bf16),
+        pltpu.VMEM((ntp, rows, feat), bf16),
+        pltpu.VMEM((ncb, rows, feat), bf16),
+        pltpu.VMEM((steps, total_rows, dfeat), bf16),
+        pltpu.VMEM((total_rows, dfeat), bf16),
+        pltpu.VMEM((total_rows, DD), f32),
+        pltpu.VMEM((steps, ntp, drows, DD), bf16),
+        pltpu.VMEM((steps, ntp, drows, DD), bf16),
+        pltpu.VMEM((steps, drows, DD), f32),
+        pltpu.VMEM((steps, ntp, drows, DD), bf16),
+        pltpu.VMEM((steps, ntp, total_rows, dfeat), bf16),
+        pltpu.VMEM((steps, ntp, total_rows, dfeat), bf16),
+        pltpu.SemaphoreType.DMA((10,)),
+        pltpu.SemaphoreType.DMA((PHASES, ntp)),
+        pltpu.SemaphoreType.DMA((PHASES, ntp)),
+    ]
+    temporal, depth = pl.pallas_call(
+        functools.partial(frame_kernel, ntp, ncb),
+        out_shape=(
+            jax.ShapeDtypeStruct((rows, feat), bf16),
+            jax.ShapeDtypeStruct((steps, total_rows, dfeat), f32),
+        ),
+        in_specs=[vmem, vmem, pl.BlockSpec(memory_space=pltpu.SMEM), vmem, vmem] + [hbm] * 8,
+        out_specs=(vmem, vmem),
+        scratch_shapes=scratch,
+        compiler_params=pltpu.CompilerParams(
+            collective_id=0, has_side_effects=True, vmem_limit_bytes=60 * 1024 * 1024
+        ),
+    )(
+        hidden_in,
+        norm_gain.reshape(1, feat),
+        lengths,
+        tokens,
+        depth_gain,
+        *big,
+    )
+    return temporal, depth.astype(bf16)
+
+
 def solution(mesh):
     in_specs = (
         P("cb", "tp"),
@@ -136,6 +548,11 @@
         P("cb", "tp", None),
     )
     out_specs = (P("cb", "tp"), P("cb", None, "tp"))
-    return jax.shard_map(
-        per_device, mesh=mesh, in_specs=in_specs, out_specs=out_specs, check_vma=False
-    )
+
+    def run(*args):
+        body = fused if fits(mesh, args[0], args[8]) else per_device
+        return jax.shard_map(
+            body, mesh=mesh, in_specs=in_specs, out_specs=out_specs, check_vma=False
+        )(*args)
+
+    return run

time: 277 us -> 88.1 us (0.32)
  waiting for transfers between devices: 133 us -> 0 us
  blocking collectives: 89.1 us -> 0 us
  Pallas kernels: 0 us -> 77 us
  matrix products: 26.5 us -> 0 us
  between operations: 14.1 us -> 0.64 us
  local copies, waits for them, and re-layouts: 0.95 us -> 8.64 us
  other arithmetic: 7.6 us -> 1.54 us
  starting transfers between devices: 5.08 us -> 0 us
    reduce_scatter x5 -> x0, waiting for transfers between devices: 127 us -> none  [the longest x2 54 us: per_device(): lax.psum_scatter(term, 'tp', scatter_dimension=1, tiled=True)]
    pallas_call x0 -> x1, Pallas kernels: none -> 77 us  [fused(): pl.pallas_call(functools.partial(frame_kernel, ntp, ncb), out_shape=(jax....]
    all_gather x4 -> x0, blocking collectives: 49.1 us -> none  [the longest x2 26.5 us: per_device(): lax.all_gather(xn_loc, 'tp', axis=1, tiled=True)]
    psum x2 -> x0, blocking collectives: 31.8 us -> none  [the longest x1 18.1 us: per_device(): sum_sq = lax.psum(jnp.sum(hid32 * hid32, axis=1), 'tp')]
    dot_general x12 -> x0, matrix products: 26.5 us -> none  [the longest x1 6.73 us: per_device(): jnp.einsum('rd,idf->rif', lax.all_gather(normed, 'tp', axis=1, tiled=True...]
    all_to_all x1 -> x0, blocking collectives: 8.12 us -> none  [per_device(): lax.all_to_all(attended, 'tp', split_axis=1, concat_axis=0, tiled=True)]
    unnamed x20 -> x3, local copies, waits for them, and re-layouts: 0.05 us -> 7.38 us
    all_to_all x1 -> x0, waiting for transfers between devices: 6.14 us -> none  [per_device(): lax.all_to_all(qkv.reshape(width_tp, per_dev, 3, feat_loc), 'tp', split_a...]
  transfers between devices with their start and end apart: 7 -> 0, of which waited for: 6 -> 0; matrix products, arithmetic and copies ran while one was open for 3% -> 0% of each run, Pallas kernels for 0% -> 0%
where the time goes in v1:
time: 88.1 us; the launch traced here: 87.8 us
  Pallas kernels  77 us (87%)
  local copies, waits for them, and re-layouts  8.64 us (10%)
  other arithmetic  1.54 us (2%)
    pallas_call x1, Pallas kernels, fused(): pl.pallas_call(functools.partial(frame_kernel, ntp, ncb), out_shape=(jax....  77 us
    unnamed x3, local copies, waits for them, and re-layouts  7.38 us

profile of v1, /device:TPU:0, one launch (start us, length us, event | category | flops | bytes accessed | tf_op | source)
XLA Modules:
  0.0 87.8 jit_solution(239803192545934495)
XLA Ops:
  0.6 1.3 %reshape.7.gain = bf16[1,512]{1,0:T(2,128)(2,1)} reshape(bf16[512]{0:T(512)(128)(2,1)} %param.14) | data formatting | bytes 2048 | tf_op jit(solution)/shard_map/reshape | solution.py:525
  1.9 1.4 %copy.15.tokens = s32[128,2]{1,0:T(8,128)} copy(s32[128,2]{0,1:T(2,128)} %param.20) | data formatting | bytes 2048 | tf_op args[7]
  3.3 4.6 %copy.16.w_gu = bf16[2,2,1024,352]{3,2,1,0:T(8,128)(2,1)} copy(bf16[2,2,1024,352]{2,3,1,0:T(8,128)(2,1)} %param.24) | data formatting | bytes 5767168 | tf_op args[11]
  7.9 77.0 %shard_map.140 = (bf16[32,512]{1,0:T(8,128)(2,1)}, f32[2,128,128]{2,1,0:T(8,128)}) custom-call(bf16[32,512]{1,0:T(8,128)(2,1)} %hid.1, bf16[1,512]{1,0:T(2,128)(2,1)} %reshape.7.gain, s32[4]{0:T(128)} %lengths.1, s32[128,2]{1,0:T(8,128)} %copy.15.tokens, bf16[2,1024]{1,0:T(2,128)(2,1)} %depth_gain.1, bf16[3,4096,512]{2,1,0:T(8,128)(2,1)} %w_qkv.1, ...), custom_call_target="tpu_custom_call" | custom-call | tf_op jit(solution)/shard_map/pallas_call | solution.py:511
  84.9 1.5 %convert_element_type.3 = bf16[2,128,128]{2,1,0:T(8,128)(2,1)} convert(f32[2,128,128]{2,1,0:T(8,128)} %get-tuple-element.5) | non-fusion elementwise | flops 32768 | bytes 196608 | tf_op jit(solution)/shard_map/convert_element_type | solution.py:531
  86.4 1.4 %copy.18 = bf16[32,512]{1,0:T(8,128)(2,1)} copy(bf16[32,512]{1,0:T(8,128)(2,1)} %get-tuple-element.8) | data formatting | bytes 65536

commit v2 on v1

--- a/solution.py
+++ b/solution.py
@@ -123,8 +123,8 @@
 
 
 MESH = pl.DeviceIdType.MESH
-NORM, GAIN, CARRY, QKV, BACK, OUT, FRAME, XSUM, XN, DOWN = 0, 1, 2, 3, 4, 5, 6, 7, 9, 11
-PHASES = 13
+NORM, GAIN, CARRY, BACK, OUT, FRAME, XSUM, XN, DOWN, QKV = 0, 1, 2, 3, 4, 5, 6, 8, 10, 12
+PHASES = 15
 
 
 def frame_kernel(
@@ -161,16 +161,19 @@
     att_send,
     att_recv,
     returned,
+    o_twin,
     o_send,
     o_recv,
     frame,
     emb,
     carried,
     part,
+    x_twin,
     x_send,
     x_recv,
     x_own,
     xn_all,
+    d_twin,
     d_send,
     d_recv,
     wsem,
@@ -188,6 +191,11 @@
     drows = frame.shape[0] * rows // ntp
     dfeat = DD // ntp
     order = sorted(range(1, ntp), key=lambda i: abs(i - ntp // 2))
+    chips = ntp // 2
+    core = lax.rem(me, 2)
+    chip = lax.div(me, 2)
+    twin = chip * 2 + 1 - core
+    far = sorted(range(1, chips), key=lambda j: abs(j - chips // 2))
 
     weights = {}
 
@@ -221,32 +229,51 @@
     def cb_at(i):
         return lax.rem(grp + i, ncb)
 
+    def same_core(j):
+        return lax.rem(chip + j, chips) * 2 + core
+
+    def share(buffers, phases):
+        direct = [
+            [put(b.at[me], b.at[me], p, j, "tp", same_core(j)) for b, p in zip(buffers, phases)]
+            for j in far
+        ]
+        passed = [put(b.at[me], b.at[me], p, chips, "tp", twin) for b, p in zip(buffers, phases)]
+        return direct, passed
+
+    def pass_on(buffers, phases, state):
+        direct, passed = state
+        for j, copies in zip(far, direct):
+            origin = same_core(chips - j)
+            for b, p, copy in zip(buffers, phases, copies):
+                copy.wait_recv()
+                passed.append(put(b.at[origin], b.at[origin], p, chips + j, "tp", twin))
+        return passed
+
     barrier = pltpu.get_barrier_semaphore()
     for i in range(1, ntp):
         pl.semaphore_signal(barrier, inc=1, device_id={"tp": tp_at(i)}, device_id_type=MESH)
     for i in range(1, ncb):
         pl.semaphore_signal(barrier, inc=1, device_id={"cb": cb_at(i)}, device_id_type=MESH)
 
-    gain32 = gain[...].astype(f32)
+    gain32 = gain[...].reshape(1, feat).astype(f32)
     gain_rows = [gain32[:, h * HEAD_DIM : (h + 1) * HEAD_DIM] for h in range(heads)]
     gain_rows.append(jnp.zeros((16 - heads, HEAD_DIM), f32))
     gain_all[me] = jnp.concatenate(gain_rows, axis=0).astype(bf16)
     hid_all[me] = hid[...]
     pl.semaphore_wait(barrier, ntp - 1 + ncb - 1)
 
-    arriving = []
-    for i in order:
-        arriving.append(put(hid_all.at[me], hid_all.at[me], NORM, i, "tp", tp_at(i)))
-        arriving.append(put(gain_all.at[me], gain_all.at[me], GAIN, i, "tp", tp_at(i)))
+    shared = share([hid_all, gain_all], [NORM, GAIN])
 
     weights["e"].wait()
-    codes = lax.broadcasted_iota(jnp.int32, (tokens.shape[0], CARD), 1)
+    codes = lax.broadcasted_iota(jnp.int32, (tokens.shape[1], CARD), 1)
     for local in range(steps):
-        one_hot = (tokens[:, local : local + 1] == codes).astype(f32).astype(bf16)
+        spread = jnp.broadcast_to(tokens[local : local + 1, :], (128, tokens.shape[1]))
+        chosen = jnp.transpose(spread)[:, 0:1]
+        one_hot = (chosen == codes).astype(f32).astype(bf16)
         emb[local] = jnp.dot(one_hot, ve[local], preferred_element_type=f32).astype(bf16)
     carry = put(emb.at[steps - 1], carried, CARRY, 1, "cb", cb_at(1))
 
-    for copy in arriving:
+    for copy in pass_on([hid_all, gain_all], [NORM, GAIN], shared):
         copy.wait_recv()
     load("k", keys, vk, 4)
     load("v", values, vv, 5)
@@ -275,6 +302,7 @@
     column = lax.broadcasted_iota(jnp.int32, (size, size), 1)
     source = ((place // per_dev) % heads) * rows + (place // blk) * per_dev + place % per_dev
     perm = (column == source).astype(f32).astype(bf16)
+    arriving = []
     for i in range(3):
         weights["q", i].wait()
         full = jnp.dot(normed[...], vq[i], preferred_element_type=f32).astype(bf16)
@@ -282,11 +310,12 @@
             [full[:, h * HEAD_DIM : (h + 1) * HEAD_DIM] for h in range(heads)], axis=0
         )
         moved = jnp.dot(perm, stacked, preferred_element_type=f32).astype(bf16)
-        qkv_send[:, i * blk : (i + 1) * blk, :] = moved.reshape(ntp, blk, HEAD_DIM)
-    arriving = [
-        put(qkv_send.at[tp_at(i)], qkv_recv.at[me], QKV, i, "tp", tp_at(i)) for i in order
-    ]
-    qkv_recv[me] = qkv_send[me]
+        qkv_send[i] = moved.reshape(ntp, blk, HEAD_DIM)
+        arriving += [
+            put(qkv_send.at[i, tp_at(j)], qkv_recv.at[i, me], QKV + i, j, "tp", tp_at(j))
+            for j in order
+        ]
+        qkv_recv[i, me] = qkv_send[i, me]
     weights["k"].wait()
     weights["v"].wait()
     for copy in arriving:
@@ -302,9 +331,9 @@
     live = (row % per_dev == col // CACHE) & (col % CACHE < count)
     head_of = lax.broadcasted_iota(jnp.int32, (blk, HEAD_DIM), 0) // per_dev
     for s in range(ntp):
-        query = qkv_recv[s, 0:blk, :].astype(f32)
-        key_new = qkv_recv[s, blk : 2 * blk, :].astype(f32)
-        value_new = qkv_recv[s, 2 * blk : 3 * blk, :].astype(f32)
+        query = qkv_recv[0, s].astype(f32)
+        key_new = qkv_recv[1, s].astype(f32)
+        value_new = qkv_recv[2, s].astype(f32)
         spread = jnp.concatenate(
             [jnp.where(head_of == h, query, 0.0) for h in range(heads)], axis=1
         ).astype(bf16)
@@ -349,19 +378,24 @@
         ).astype(bf16)
 
     weights["o"].wait()
+
+    def projected(device):
+        cols = pl.ds(pl.multiple_of(device * feat, feat), feat)
+        return jnp.dot(returned[...], vo[:, cols], preferred_element_type=f32)
+
+    for z in range(chips):
+        o_twin[0, z] = projected(2 * z + 1 - core).astype(bf16)
+    merged = put(o_twin.at[0], o_twin.at[1], OUT, 0, "tp", twin)
+    mine = [projected(same_core(j)) for j in far + [0]]
+    merged.wait_recv()
     arriving = []
-    for i in order + [0]:
-        cols = pl.ds(pl.multiple_of(tp_at(i) * feat, feat), feat)
-        term = jnp.dot(returned[...], vo[:, cols], preferred_element_type=f32)
-        if i == 0:
-            attn = term
-        else:
-            o_send[i] = term.astype(bf16)
-            arriving.append(put(o_send.at[i], o_recv.at[i], OUT, i, "tp", tp_at(i)))
-    for copy in arriving:
+    for j, term in zip(far, mine):
+        o_send[j] = (term + o_twin[1, lax.rem(chip + j, chips)].astype(f32)).astype(bf16)
+        arriving.append(put(o_send.at[j], o_recv.at[j], OUT, j, "tp", same_core(j)))
+    attn = mine[-1] + o_twin[1, chip].astype(f32)
+    for j, copy in zip(far, arriving):
         copy.wait_recv()
-    for i in range(1, ntp):
-        attn = attn + o_recv[i].astype(f32)
+        attn = attn + o_recv[j].astype(f32)
     temporal = (hid[...].astype(f32) + attn).astype(bf16)
     out_t[...] = temporal
     frame[grp] = temporal
@@ -375,72 +409,99 @@
         copy.wait_recv()
     lhs = frame[...].reshape(ncb * rows, feat)
 
+    own_cols = pl.ds(pl.multiple_of(me * dfeat, dfeat), dfeat)
+
+    def rows_of(device):
+        return pl.ds(pl.multiple_of(device * drows, drows), drows)
+
+    def cols_of(device):
+        return pl.ds(pl.multiple_of(device * dfeat, dfeat), dfeat)
+
+    merged = []
+    for local in range(steps):
+        part[local] = jnp.dot(lhs, vi[local], preferred_element_type=f32)
+        before = carried[...] if local == 0 else emb[local - 1]
+        part[local, :, own_cols] = part[local, :, own_cols] + before.astype(f32)
+        for z in range(chips):
+            x_twin[local, 0, z] = part[local, rows_of(2 * z + 1 - core), :].astype(bf16)
+        merged.append(
+            put(x_twin.at[local, 0], x_twin.at[local, 1], XSUM + local, 0, "tp", twin)
+        )
     arriving = []
-    own_cols = pl.ds(pl.multiple_of(me * dfeat, dfeat), dfeat)
     for local in range(steps):
-        part[...] = jnp.dot(lhs, vi[local], preferred_element_type=f32)
-        before = carried[...] if local == 0 else emb[local - 1]
-        part[:, own_cols] = part[:, own_cols] + before.astype(f32)
-        x_send[local] = part[...].astype(bf16).reshape(ntp, drows, DD)
-        arriving.append(
-            [
-                put(
-                    x_send.at[local, tp_at(i)], x_recv.at[local, i], XSUM + local, i, "tp", tp_at(i)
-                )
-                for i in order
-            ]
-        )
-        own_rows = pl.ds(pl.multiple_of(me * drows, drows), drows)
-        x_own[local] = part[own_rows, :]
+        merged[local].wait_recv()
+        copies = []
+        for j in far:
+            x_send[local, j] = (
+                part[local, rows_of(same_core(j)), :]
+                + x_twin[local, 1, lax.rem(chip + j, chips)].astype(f32)
+            ).astype(bf16)
+            copies.append(
+                put(x_send.at[local, j], x_recv.at[local, j], XSUM + local, j, "tp", same_core(j))
+            )
+        arriving.append(copies)
     gathers = []
     for local in range(steps):
-        for copy in arriving[local]:
+        x = part[local, rows_of(me), :] + x_twin[local, 1, chip].astype(f32)
+        for j, copy in zip(far, arriving[local]):
             copy.wait_recv()
-        x = x_own[local]
-        for i in range(1, ntp):
-            x = x + x_recv[local, i].astype(f32)
+            x = x + x_recv[local, j].astype(f32)
         x_own[local] = x
         inv = lax.rsqrt(jnp.sum(x * x, axis=1, keepdims=True) / DD + eps)
         gains = depth_gain[local : local + 1, :].astype(f32)
         xn_all[local, me] = (x * inv * gains).astype(bf16)
-        gathers.append(
-            [
-                put(xn_all.at[local, me], xn_all.at[local, me], XN + local, i, "tp", tp_at(i))
-                for i in order
-            ]
-        )
+        gathers.append(share([xn_all.at[local]], [XN + local]))
 
     weights["g"].wait()
     weights["d"].wait()
-    arriving = []
+    contract_last = (((1,), (1,)), ((), ()))
+    for local in range(steps):
+        gathers[local] = pass_on([xn_all.at[local]], [XN + local], gathers[local])
+    merged, summed = [], []
+
+    def send_down(local):
+        merged[local].wait_recv()
+        copies = []
+        for j in far:
+            d_send[local, j] = (
+                part[local, :, cols_of(same_core(j))]
+                + d_twin[local, 1, lax.rem(chip + j, chips)].astype(f32)
+            ).astype(bf16)
+            copies.append(
+                put(d_send.at[local, j], d_recv.at[local, j], DOWN + local, j, "tp", same_core(j))
+            )
+        summed.append(copies)
+
     for local in range(steps):
         for copy in gathers[local]:
             copy.wait_recv()
         lhs = xn_all[local].reshape(ntp * drows, DD)
-        gate = jnp.dot(lhs, vg[local, 0], preferred_element_type=f32)
-        upper = jnp.dot(lhs, vg[local, 1], preferred_element_type=f32)
+        gate = lax.dot_general(lhs, vg[local, 0], contract_last, preferred_element_type=f32)
+        upper = lax.dot_general(lhs, vg[local, 1], contract_last, preferred_element_type=f32)
         act = (jax.nn.silu(gate) * upper).astype(bf16)
-        part[...] = jnp.dot(act, vd[local], preferred_element_type=f32)
-        own_rows = pl.ds(pl.multiple_of(me * drows, drows), drows)
-        part[own_rows, :] = part[own_rows, :] + x_own[local]
-        copies = []
-        for i in order:
-            cols = pl.ds(pl.multiple_of(tp_at(i) * dfeat, dfeat), dfeat)
-            d_send[local, i] = part[:, cols].astype(bf16)
-            copies.append(
-                put(d_send.at[local, i], d_recv.at[local, i], DOWN + local, i, "tp", tp_at(i))
-            )
-        arriving.append(copies)
-        out_d[local] = part[:, own_cols]
+        part[local] = jnp.dot(act, vd[local], preferred_element_type=f32)
+        part[local, rows_of(me), :] = part[local, rows_of(me), :] + x_own[local]
+        for z in range(chips):
+            d_twin[local, 0, z] = part[local, :, cols_of(2 * z + 1 - core)].astype(bf16)
+        merged.append(
+            put(d_twin.at[local, 0], d_twin.at[local, 1], DOWN + local, 0, "tp", twin)
+        )
+        if local:
+            send_down(local - 1)
+    send_down(steps - 1)
     for local in range(steps):
-        for copy in arriving[local]:
+        y = part[local, :, own_cols] + d_twin[local, 1, chip].astype(f32)
+        for j, copy in zip(far, summed[local]):
             copy.wait_recv()
-        y = out_d[local]
-        for i in range(1, ntp):
-            y = y + d_recv[local, i].astype(f32)
-        out_d[local] = y
+            y = y + d_recv[local, j].astype(f32)
+        out_d[local] = y.astype(out_d.dtype)
     for copy in sent:
         copy.wait_send()
+
+
+def finish(temporal, depth, out_t, out_d):
+    out_t[...] = temporal[...]
+    out_d[...] = depth[...]
 
 
 def fits(mesh, hidden_in, w_in):
@@ -449,6 +510,8 @@
     steps = w_in.shape[0] // ncb
     return (
         steps == 2
+        and ntp % 2 == 0
+        and rows * ncb == 128
         and feat % HEAD_DIM == 0
         and feat // HEAD_DIM <= 16
         and rows % ntp == 0
@@ -478,32 +541,36 @@
     rows, feat = hidden_in.shape
     blk = rows // ntp * (feat // HEAD_DIM)
     steps = w_in.shape[0]
+    chips = ntp // 2
     total_rows = rows * ncb
     drows, dfeat = total_rows // ntp, DD // ntp
     vmem = pl.BlockSpec(memory_space=pltpu.VMEM)
     hbm = pl.BlockSpec(memory_space=pl.ANY)
-    big = [w_qkv, w_out, cache_keys, cache_values, w_in, embed, w_gate_up, w_down]
+    big = [w_qkv, w_out, cache_keys, cache_values, w_in, embed, jnp.swapaxes(w_gate_up, 2, 3), w_down]
     scratch = [pltpu.VMEM(a.shape, a.dtype) for a in big] + [
         pltpu.VMEM((ntp, rows, feat), bf16),
         pltpu.VMEM((ntp, 16, HEAD_DIM), bf16),
         pltpu.VMEM((rows, D), bf16),
-        pltpu.VMEM((ntp, 3 * blk, HEAD_DIM), bf16),
-        pltpu.VMEM((ntp, 3 * blk, HEAD_DIM), bf16),
+        pltpu.VMEM((3, ntp, blk, HEAD_DIM), bf16),
+        pltpu.VMEM((3, ntp, blk, HEAD_DIM), bf16),
         pltpu.VMEM((ntp, blk, HEAD_DIM), bf16),
         pltpu.VMEM((ntp, blk, HEAD_DIM), bf16),
         pltpu.VMEM((rows, feat), bf16),
-        pltpu.VMEM((ntp, rows, feat), bf16),
-        pltpu.VMEM((ntp, rows, feat), bf16),
+        pltpu.VMEM((2, chips, rows, feat), bf16),
+        pltpu.VMEM((chips, rows, feat), bf16),
+        pltpu.VMEM((chips, rows, feat), bf16),
         pltpu.VMEM((ncb, rows, feat), bf16),
         pltpu.VMEM((steps, total_rows, dfeat), bf16),
         pltpu.VMEM((total_rows, dfeat), bf16),
-        pltpu.VMEM((total_rows, DD), f32),
-        pltpu.VMEM((steps, ntp, drows, DD), bf16),
-        pltpu.VMEM((steps, ntp, drows, DD), bf16),
+        pltpu.VMEM((steps, total_rows, DD), f32),
+        pltpu.VMEM((steps, 2, chips, drows, DD), bf16),
+        pltpu.VMEM((steps, chips, drows, DD), bf16),
+        pltpu.VMEM((steps, chips, drows, DD), bf16),
         pltpu.VMEM((steps, drows, DD), f32),
         pltpu.VMEM((steps, ntp, drows, DD), bf16),
-        pltpu.VMEM((steps, ntp, total_rows, dfeat), bf16),
-        pltpu.VMEM((steps, ntp, total_rows, dfeat), bf16),
+        pltpu.VMEM((steps, 2, chips, total_rows, dfeat), bf16),
+        pltpu.VMEM((steps, chips, total_rows, dfeat), bf16),
+        pltpu.VMEM((steps, chips, total_rows, dfeat), bf16),
         pltpu.SemaphoreType.DMA((10,)),
         pltpu.SemaphoreType.DMA((PHASES, ntp)),
         pltpu.SemaphoreType.DMA((PHASES, ntp)),
@@ -512,7 +579,7 @@
         functools.partial(frame_kernel, ntp, ncb),
         out_shape=(
             jax.ShapeDtypeStruct((rows, feat), bf16),
-            jax.ShapeDtypeStruct((steps, total_rows, dfeat), f32),
+            jax.ShapeDtypeStruct((steps, total_rows, dfeat), bf16),
         ),
         in_specs=[vmem, vmem, pl.BlockSpec(memory_space=pltpu.SMEM), vmem, vmem] + [hbm] * 8,
         out_specs=(vmem, vmem),
@@ -522,13 +589,21 @@
         ),
     )(
         hidden_in,
-        norm_gain.reshape(1, feat),
+        norm_gain,
         lengths,
-        tokens,
+        tokens.T,
         depth_gain,
         *big,
     )
-    return temporal, depth.astype(bf16)
+    return pl.pallas_call(
+        finish,
+        out_shape=(
+            jax.ShapeDtypeStruct(temporal.shape, bf16),
+            jax.ShapeDtypeStruct(depth.shape, bf16),
+        ),
+        in_specs=[vmem, vmem],
+        out_specs=(vmem, vmem),
+    )(temporal, depth)
 
 
 def solution(mesh):

time: 88.1 us -> 66.3 us (0.75)
  Pallas kernels: 77 us -> 65.4 us
  local copies, waits for them, and re-layouts: 8.64 us -> 0 us
  other arithmetic: 1.54 us -> 0 us
    pallas_call x1, Pallas kernels: 77 us -> 63.9 us  [fused(): pl.pallas_call(functools.partial(frame_kernel, ntp, ncb), out_shape=(jax....]
    unnamed x3 -> x0, local copies, waits for them, and re-layouts: 7.38 us -> none
    convert_element_type x1 -> x0, other arithmetic: 1.54 us -> none  [fused(): return (temporal, depth.astype(bf16))]
    pallas_call x0 -> x1, Pallas kernels: none -> 1.5 us  [fused(): pl.pallas_call(finish, out_shape=(jax.ShapeDtypeStruct(temporal.shape, bf...]
    reshape x1 -> x0, local copies, waits for them, and re-layouts: 1.26 us -> none  [fused(): norm_gain.reshape(1, feat)]
where the time goes in v2:
time: 66.3 us; the launch traced here: 66.1 us
  Pallas kernels  65.4 us (99%)
    pallas_call x1, Pallas kernels, fused(): pl.pallas_call(functools.partial(frame_kernel, ntp, ncb), out_shape=(jax....  63.9 us
    pallas_call x1, Pallas kernels, fused(): pl.pallas_call(finish, out_shape=(jax.ShapeDtypeStruct(temporal.shape, bf...  1.5 us

profile of v2, /device:TPU:0, one launch (start us, length us, event | category | flops | bytes accessed | tf_op | source)
XLA Modules:
  0.0 66.1 jit_solution(15842613828986224854)
XLA Ops:
  0.6 63.9 %shard_map.140 = (bf16[32,512]{1,0:T(8,128)(2,1)}, bf16[2,128,128]{2,1,0:T(8,128)(2,1)}) custom-call(bf16[32,512]{1,0:T(8,128)(2,1)} %hid.1, bf16[512]{0:T(512)(128)(2,1)} %gain.1, s32[4]{0:T(128)} %lengths.1, s32[2,128]{1,0:T(2,128)} %bitcast.3, bf16[2,1024]{1,0:T(2,128)(2,1)} %depth_gain.1, bf16[3,4096,512]{2,1,0:T(8,128)(2,1)} %w_qkv.1, ...), custom_call_target="tpu_custom_call" | custom-call | tf_op jit(solution)/shard_map/pallas_call | solution.py:578
  64.6 1.5 %shard_map.141 = (bf16[32,512]{1,0:T(8,128)(2,1)}, bf16[2,128,128]{2,1,0:T(8,128)(2,1)}) custom-call(bf16[32,512]{1,0:T(8,128)(2,1)} %get-tuple-element.4.temporal, bf16[2,128,128]{2,1,0:T(8,128)(2,1)} %get-tuple-element.5.depth), custom_call_target="tpu_custom_call" | custom-call | tf_op jit(solution)/shard_map/pallas_call | solution.py:598

commit v3 on v2

--- a/solution.py
+++ b/solution.py
@@ -155,7 +155,7 @@
     vd,
     hid_all,
     gain_all,
-    normed,
+    acc,
     qkv_send,
     qkv_recv,
     att_send,
@@ -204,9 +204,6 @@
         copy.start()
         weights[name] = copy
 
-    for i in range(3):
-        load(("q", i), w_qkv.at[i], vq.at[i], i)
-    load("e", embed, ve, 3)
 
     sent = []
 
@@ -255,6 +252,16 @@
     for i in range(1, ncb):
         pl.semaphore_signal(barrier, inc=1, device_id={"cb": cb_at(i)}, device_id_type=MESH)
 
+    def part_of(device):
+        return pl.ds(pl.multiple_of(device * feat, feat), feat)
+
+    visits = [me, twin]
+    visits += [same_core(chips - j) for j in far]
+    visits += [same_core(chips - j) + 1 - 2 * core for j in far]
+    for n, origin in enumerate(visits):
+        load(
+            ("q", n), w_qkv.at[:, part_of(origin), :], vq.at[:, part_of(origin), :], n
+        )
     gain32 = gain[...].reshape(1, feat).astype(f32)
     gain_rows = [gain32[:, h * HEAD_DIM : (h + 1) * HEAD_DIM] for h in range(heads)]
     gain_rows.append(jnp.zeros((16 - heads, HEAD_DIM), f32))
@@ -262,7 +269,70 @@
     hid_all[me] = hid[...]
     pl.semaphore_wait(barrier, ntp - 1 + ncb - 1)
 
-    shared = share([hid_all, gain_all], [NORM, GAIN])
+    buffers, phases = [hid_all, gain_all], [NORM, GAIN]
+    direct, passed = share(buffers, phases)
+    relayed = []
+    total = jnp.zeros((rows, 1), f32)
+
+    size = rows * heads
+    place = lax.broadcasted_iota(jnp.int32, (size, size), 0)
+    column = lax.broadcasted_iota(jnp.int32, (size, size), 1)
+    source = ((place // per_dev) % heads) * rows + (place // blk) * per_dev + place % per_dev
+    perm = (column == source).astype(f32).astype(bf16)
+    arriving = []
+    for n, origin in enumerate(visits):
+        if n == 1:
+            for copy in passed:
+                copy.wait_recv()
+        elif 2 <= n < 1 + chips:
+            relayed.append([])
+            for b, p, copy in zip(buffers, phases, direct[n - 2]):
+                copy.wait_recv()
+                relayed[-1].append(
+                    put(b.at[origin], b.at[origin], p, chips + far[n - 2], "tp", twin)
+                )
+        elif n >= 1 + chips:
+            for copy in relayed[n - 1 - chips]:
+                copy.wait_recv()
+        piece = hid_all[origin].astype(f32)
+        gains = gain_all[origin].astype(f32)
+        total = total + jnp.sum(piece * piece, axis=1, keepdims=True)
+        scaled = jnp.concatenate(
+            [
+                piece[:, h * HEAD_DIM : (h + 1) * HEAD_DIM] * gains[h : h + 1, :]
+                for h in range(heads)
+            ],
+            axis=1,
+        ).astype(bf16)
+        weights["q", n].wait()
+        if n == 4:
+            load("e", embed, ve, ntp)
+            load("k", keys, vk, ntp + 1)
+            load("v", values, vv, ntp + 2)
+        if n == 6:
+            load("o", w_out, vo, ntp + 3)
+            load("i", w_in, vi, ntp + 4)
+            load("g", w_gu, vg, ntp + 5)
+            load("d", w_down, vd, ntp + 6)
+        inv = lax.rsqrt(total / D + eps)
+        for i in range(3):
+            term = jnp.dot(scaled, vq[i, part_of(origin), :], preferred_element_type=f32)
+            if n:
+                term = term + acc[i]
+            if n < ntp - 1:
+                acc[i] = term
+                continue
+            full = (term * inv).astype(bf16)
+            stacked = jnp.concatenate(
+                [full[:, h * HEAD_DIM : (h + 1) * HEAD_DIM] for h in range(heads)], axis=0
+            )
+            moved = jnp.dot(perm, stacked, preferred_element_type=f32).astype(bf16)
+            qkv_send[i] = moved.reshape(ntp, blk, HEAD_DIM)
+            arriving += [
+                put(qkv_send.at[i, tp_at(j)], qkv_recv.at[i, me], QKV + i, j, "tp", tp_at(j))
+                for j in order
+            ]
+            qkv_recv[i, me] = qkv_send[i, me]
 
     weights["e"].wait()
     codes = lax.broadcasted_iota(jnp.int32, (tokens.shape[1], CARD), 1)
@@ -272,50 +342,6 @@
         one_hot = (chosen == codes).astype(f32).astype(bf16)
         emb[local] = jnp.dot(one_hot, ve[local], preferred_element_type=f32).astype(bf16)
     carry = put(emb.at[steps - 1], carried, CARRY, 1, "cb", cb_at(1))
-
-    for copy in pass_on([hid_all, gain_all], [NORM, GAIN], shared):
-        copy.wait_recv()
-    load("k", keys, vk, 4)
-    load("v", values, vv, 5)
-    load("o", w_out, vo, 6)
-    load("i", w_in, vi, 7)
-    load("g", w_gu, vg, 8)
-    load("d", w_down, vd, 9)
-
-    total = jnp.zeros((rows, 1), f32)
-    for s in range(ntp):
-        piece = hid_all[s].astype(f32)
-        total = total + jnp.sum(piece * piece, axis=1, keepdims=True)
-    inv = lax.rsqrt(total / D + eps)
-    for s in range(ntp):
-        piece = hid_all[s].astype(f32)
-        gains = gain_all[s].astype(f32)
-        for h in range(heads):
-            cols = slice(h * HEAD_DIM, (h + 1) * HEAD_DIM)
-            at = s * feat + h * HEAD_DIM
-            normed[:, at : at + HEAD_DIM] = (
-                piece[:, cols] * inv * gains[h : h + 1, :]
-            ).astype(bf16)
-
-    size = rows * heads
-    place = lax.broadcasted_iota(jnp.int32, (size, size), 0)
-    column = lax.broadcasted_iota(jnp.int32, (size, size), 1)
-    source = ((place // per_dev) % heads) * rows + (place // blk) * per_dev + place % per_dev
-    perm = (column == source).astype(f32).astype(bf16)
-    arriving = []
-    for i in range(3):
-        weights["q", i].wait()
-        full = jnp.dot(normed[...], vq[i], preferred_element_type=f32).astype(bf16)
-        stacked = jnp.concatenate(
-            [full[:, h * HEAD_DIM : (h + 1) * HEAD_DIM] for h in range(heads)], axis=0
-        )
-        moved = jnp.dot(perm, stacked, preferred_element_type=f32).astype(bf16)
-        qkv_send[i] = moved.reshape(ntp, blk, HEAD_DIM)
-        arriving += [
-            put(qkv_send.at[i, tp_at(j)], qkv_recv.at[i, me], QKV + i, j, "tp", tp_at(j))
-            for j in order
-        ]
-        qkv_recv[i, me] = qkv_send[i, me]
     weights["k"].wait()
     weights["v"].wait()
     for copy in arriving:
@@ -330,21 +356,27 @@
         count = jnp.where(col // CACHE == r, lengths[r], count)
     live = (row % per_dev == col // CACHE) & (col % CACHE < count)
     head_of = lax.broadcasted_iota(jnp.int32, (blk, HEAD_DIM), 0) // per_dev
+    queries, products = [], []
     for s in range(ntp):
         query = qkv_recv[0, s].astype(f32)
-        key_new = qkv_recv[1, s].astype(f32)
-        value_new = qkv_recv[2, s].astype(f32)
         spread = jnp.concatenate(
             [jnp.where(head_of == h, query, 0.0) for h in range(heads)], axis=1
         ).astype(bf16)
         cols = slice(s * feat, (s + 1) * feat)
         old_keys = vk[:, :, cols].reshape(slots, feat)
-        scores = (
+        products.append(
             lax.dot_general(
-                spread, old_keys, (((1,), (1,)), ((), ())), preferred_element_type=f32
+                old_keys, spread, (((1,), (1,)), ((), ())), preferred_element_type=f32
             )
-            * scale
         )
+        queries.append(query)
+    products = jnp.transpose(jnp.concatenate(products, axis=1))
+    for s in range(ntp):
+        query = queries[s]
+        key_new = qkv_recv[1, s].astype(f32)
+        value_new = qkv_recv[2, s].astype(f32)
+        cols = slice(s * feat, (s + 1) * feat)
+        scores = products[s * blk : (s + 1) * blk, :] * scale
         scores = jnp.where(live, scores, -1e30)
         fresh = jnp.sum(query * key_new, axis=1, keepdims=True) * scale
         top = jnp.maximum(jnp.max(scores, axis=1, keepdims=True), fresh)
@@ -455,8 +487,7 @@
     weights["g"].wait()
     weights["d"].wait()
     contract_last = (((1,), (1,)), ((), ()))
-    for local in range(steps):
-        gathers[local] = pass_on([xn_all.at[local]], [XN + local], gathers[local])
+    gathers[0] = pass_on([xn_all.at[0]], [XN], gathers[0])
     merged, summed = [], []
 
     def send_down(local):
@@ -479,6 +510,10 @@
         gate = lax.dot_general(lhs, vg[local, 0], contract_last, preferred_element_type=f32)
         upper = lax.dot_general(lhs, vg[local, 1], contract_last, preferred_element_type=f32)
         act = (jax.nn.silu(gate) * upper).astype(bf16)
+        if local + 1 < steps:
+            gathers[local + 1] = pass_on(
+                [xn_all.at[local + 1]], [XN + local + 1], gathers[local + 1]
+            )
         part[local] = jnp.dot(act, vd[local], preferred_element_type=f32)
         part[local, rows_of(me), :] = part[local, rows_of(me), :] + x_own[local]
         for z in range(chips):
@@ -512,6 +547,7 @@
         steps == 2
         and ntp % 2 == 0
         and rows * ncb == 128
+        and ntp == 8
         and feat % HEAD_DIM == 0
         and feat // HEAD_DIM <= 16
         and rows % ntp == 0
@@ -550,7 +586,7 @@
     scratch = [pltpu.VMEM(a.shape, a.dtype) for a in big] + [
         pltpu.VMEM((ntp, rows, feat), bf16),
         pltpu.VMEM((ntp, 16, HEAD_DIM), bf16),
-        pltpu.VMEM((rows, D), bf16),
+        pltpu.VMEM((3, rows, feat), f32),
         pltpu.VMEM((3, ntp, blk, HEAD_DIM), bf16),
         pltpu.VMEM((3, ntp, blk, HEAD_DIM), bf16),
         pltpu.VMEM((ntp, blk, HEAD_DIM), bf16),
@@ -571,7 +607,7 @@
         pltpu.VMEM((steps, 2, chips, total_rows, dfeat), bf16),
         pltpu.VMEM((steps, chips, total_rows, dfeat), bf16),
         pltpu.VMEM((steps, chips, total_rows, dfeat), bf16),
-        pltpu.SemaphoreType.DMA((10,)),
+        pltpu.SemaphoreType.DMA((ntp + 7,)),
         pltpu.SemaphoreType.DMA((PHASES, ntp)),
         pltpu.SemaphoreType.DMA((PHASES, ntp)),
     ]

time: 66.3 us -> 62.1 us (0.937)
  Pallas kernels: 65.4 us -> 61.2 us
    pallas_call x1, Pallas kernels: 63.9 us -> 59.7 us  [fused(): pl.pallas_call(functools.partial(frame_kernel, ntp, ncb), out_shape=(jax....]
where the time goes in v3:
time: 62.1 us; the launch traced here: 61.9 us
  Pallas kernels  61.2 us (99%)
  between operations  0.64 us (1%)
    pallas_call x1, Pallas kernels, fused(): pl.pallas_call(functools.partial(frame_kernel, ntp, ncb), out_shape=(jax....  59.7 us
    pallas_call x1, Pallas kernels, fused(): pl.pallas_call(finish, out_shape=(jax.ShapeDtypeStruct(temporal.shape, bf...  1.5 us

profile of v3, /device:TPU:0, one launch (start us, length us, event | category | flops | bytes accessed | tf_op | source)
XLA Modules:
  0.0 61.9 jit_solution(10984836346106974581)
XLA Ops:
  0.6 59.7 %shard_map.140 = (bf16[32,512]{1,0:T(8,128)(2,1)}, bf16[2,128,128]{2,1,0:T(8,128)(2,1)}) custom-call(bf16[32,512]{1,0:T(8,128)(2,1)} %hid.1, bf16[512]{0:T(512)(128)(2,1)} %gain.1, s32[4]{0:T(128)} %lengths.1, s32[2,128]{1,0:T(2,128)} %bitcast.3, bf16[2,1024]{1,0:T(2,128)(2,1)} %depth_gain.1, bf16[3,4096,512]{2,1,0:T(8,128)(2,1)} %w_qkv.1, ...), custom_call_target="tpu_custom_call" | custom-call | tf_op jit(solution)/shard_map/pallas_call | solution.py:614
  60.3 1.5 %shard_map.141 = (bf16[32,512]{1,0:T(8,128)(2,1)}, bf16[2,128,128]{2,1,0:T(8,128)(2,1)}) custom-call(bf16[32,512]{1,0:T(8,128)(2,1)} %get-tuple-element.4.temporal, bf16[2,128,128]{2,1,0:T(8,128)(2,1)} %get-tuple-element.5.depth), custom_call_target="tpu_custom_call" | custom-call | tf_op jit(solution)/shard_map/pallas_call | solution.py:634

commit v4 on v3

--- a/solution.py
+++ b/solution.py
@@ -507,13 +507,15 @@
         for copy in gathers[local]:
             copy.wait_recv()
         lhs = xn_all[local].reshape(ntp * drows, DD)
-        gate = lax.dot_general(lhs, vg[local, 0], contract_last, preferred_element_type=f32)
-        upper = lax.dot_general(lhs, vg[local, 1], contract_last, preferred_element_type=f32)
-        act = (jax.nn.silu(gate) * upper).astype(bf16)
+        gate = lax.dot_general(vg[local, 0], lhs, contract_last, preferred_element_type=f32)
+        upper = lax.dot_general(vg[local, 1], lhs, contract_last, preferred_element_type=f32)
+        act = jnp.transpose(jax.nn.silu(gate) * upper).astype(bf16)
         if local + 1 < steps:
             gathers[local + 1] = pass_on(
                 [xn_all.at[local + 1]], [XN + local + 1], gathers[local + 1]
             )
+        if local:
+            send_down(local - 1)
         part[local] = jnp.dot(act, vd[local], preferred_element_type=f32)
         part[local, rows_of(me), :] = part[local, rows_of(me), :] + x_own[local]
         for z in range(chips):
@@ -521,8 +523,6 @@
         merged.append(
             put(d_twin.at[local, 0], d_twin.at[local, 1], DOWN + local, 0, "tp", twin)
         )
-        if local:
-            send_down(local - 1)
     send_down(steps - 1)
     for local in range(steps):
         y = part[local, :, own_cols] + d_twin[local, 1, chip].astype(f32)

time: 62.1 us -> 61.8 us (level)
  no operation moved by 1% of the time
where the time goes in v4:
time: 61.8 us; the launch traced here: 61.6 us
  Pallas kernels  60.9 us (99%)
  between operations  0.64 us (1%)
    pallas_call x1, Pallas kernels, fused(): pl.pallas_call(functools.partial(frame_kernel, ntp, ncb), out_shape=(jax....  59.4 us
    pallas_call x1, Pallas kernels, fused(): pl.pallas_call(finish, out_shape=(jax.ShapeDtypeStruct(temporal.shape, bf...  1.5 us

profile of v4, /device:TPU:0, one launch (start us, length us, event | category | flops | bytes accessed | tf_op | source)
XLA Modules:
  0.0 61.6 jit_solution(16311971839614560749)
XLA Ops:
  0.6 59.4 %shard_map.140 = (bf16[32,512]{1,0:T(8,128)(2,1)}, bf16[2,128,128]{2,1,0:T(8,128)(2,1)}) custom-call(bf16[32,512]{1,0:T(8,128)(2,1)} %hid.1, bf16[512]{0:T(512)(128)(2,1)} %gain.1, s32[4]{0:T(128)} %lengths.1, s32[2,128]{1,0:T(2,128)} %bitcast.3, bf16[2,1024]{1,0:T(2,128)(2,1)} %depth_gain.1, bf16[3,4096,512]{2,1,0:T(8,128)(2,1)} %w_qkv.1, ...), custom_call_target="tpu_custom_call" | custom-call | tf_op jit(solution)/shard_map/pallas_call | solution.py:614
  60.1 1.5 %shard_map.141 = (bf16[32,512]{1,0:T(8,128)(2,1)}, bf16[2,128,128]{2,1,0:T(8,128)(2,1)}) custom-call(bf16[32,512]{1,0:T(8,128)(2,1)} %get-tuple-element.4.temporal, bf16[2,128,128]{2,1,0:T(8,128)(2,1)} %get-tuple-element.5.depth), custom_call_target="tpu_custom_call" | custom-call | tf_op jit(solution)/shard_map/pallas_call | solution.py:634

commit v5 on v4

--- a/solution.py
+++ b/solution.py
@@ -124,7 +124,7 @@
 
 MESH = pl.DeviceIdType.MESH
 NORM, GAIN, CARRY, BACK, OUT, FRAME, XSUM, XN, DOWN, QKV = 0, 1, 2, 3, 4, 5, 6, 8, 10, 12
-PHASES = 15
+PHASES = 13
 
 
 def frame_kernel(
@@ -279,7 +279,6 @@
     column = lax.broadcasted_iota(jnp.int32, (size, size), 1)
     source = ((place // per_dev) % heads) * rows + (place // blk) * per_dev + place % per_dev
     perm = (column == source).astype(f32).astype(bf16)
-    arriving = []
     for n, origin in enumerate(visits):
         if n == 1:
             for copy in passed:
@@ -328,19 +327,21 @@
             )
             moved = jnp.dot(perm, stacked, preferred_element_type=f32).astype(bf16)
             qkv_send[i] = moved.reshape(ntp, blk, HEAD_DIM)
-            arriving += [
-                put(qkv_send.at[i, tp_at(j)], qkv_recv.at[i, me], QKV + i, j, "tp", tp_at(j))
-                for j in order
-            ]
-            qkv_recv[i, me] = qkv_send[i, me]
+    arriving = [
+        put(qkv_send.at[:, tp_at(j)], qkv_recv.at[:, me], QKV, j, "tp", tp_at(j)) for j in order
+    ]
+    qkv_recv[:, me] = qkv_send[:, me]
 
     weights["e"].wait()
     codes = lax.broadcasted_iota(jnp.int32, (tokens.shape[1], CARD), 1)
-    for local in range(steps):
+
+    def embed_tokens(local):
         spread = jnp.broadcast_to(tokens[local : local + 1, :], (128, tokens.shape[1]))
         chosen = jnp.transpose(spread)[:, 0:1]
         one_hot = (chosen == codes).astype(f32).astype(bf16)
         emb[local] = jnp.dot(one_hot, ve[local], preferred_element_type=f32).astype(bf16)
+
+    embed_tokens(steps - 1)
     carry = put(emb.at[steps - 1], carried, CARRY, 1, "cb", cb_at(1))
     weights["k"].wait()
     weights["v"].wait()
@@ -435,6 +436,8 @@
     arriving = [
         put(frame.at[grp], frame.at[grp], FRAME, i, "cb", cb_at(i)) for i in range(1, ncb)
     ]
+    for local in range(steps - 1):
+        embed_tokens(local)
     weights["i"].wait()
     carry.wait_recv()
     for copy in arriving:
@@ -449,18 +452,9 @@
     def cols_of(device):
         return pl.ds(pl.multiple_of(device * dfeat, dfeat), dfeat)
 
-    merged = []
-    for local in range(steps):
-        part[local] = jnp.dot(lhs, vi[local], preferred_element_type=f32)
-        before = carried[...] if local == 0 else emb[local - 1]
-        part[local, :, own_cols] = part[local, :, own_cols] + before.astype(f32)
-        for z in range(chips):
-            x_twin[local, 0, z] = part[local, rows_of(2 * z + 1 - core), :].astype(bf16)
-        merged.append(
-            put(x_twin.at[local, 0], x_twin.at[local, 1], XSUM + local, 0, "tp", twin)
-        )
-    arriving = []
-    for local in range(steps):
+    merged, arriving = [], []
+
+    def send_input(local):
         merged[local].wait_recv()
         copies = []
         for j in far:
@@ -472,6 +466,19 @@
                 put(x_send.at[local, j], x_recv.at[local, j], XSUM + local, j, "tp", same_core(j))
             )
         arriving.append(copies)
+
+    for local in range(steps):
+        part[local] = jnp.dot(lhs, vi[local], preferred_element_type=f32)
+        before = carried[...] if local == 0 else emb[local - 1]
+        part[local, :, own_cols] = part[local, :, own_cols] + before.astype(f32)
+        if local:
+            send_input(local - 1)
+        for z in range(chips):
+            x_twin[local, 0, z] = part[local, rows_of(2 * z + 1 - core), :].astype(bf16)
+        merged.append(
+            put(x_twin.at[local, 0], x_twin.at[local, 1], XSUM + local, 0, "tp", twin)
+        )
+    send_input(steps - 1)
     gathers = []
     for local in range(steps):
         x = part[local, rows_of(me), :] + x_twin[local, 1, chip].astype(f32)
@@ -524,13 +531,16 @@
             put(d_twin.at[local, 0], d_twin.at[local, 1], DOWN + local, 0, "tp", twin)
         )
     send_down(steps - 1)
+    early = len(sent) - len(far) * steps
+    for copy in sent[:early]:
+        copy.wait_send()
     for local in range(steps):
         y = part[local, :, own_cols] + d_twin[local, 1, chip].astype(f32)
         for j, copy in zip(far, summed[local]):
             copy.wait_recv()
             y = y + d_recv[local, j].astype(f32)
         out_d[local] = y.astype(out_d.dtype)
-    for copy in sent:
+    for copy in sent[early:]:
         copy.wait_send()
 
 

time: 61.8 us -> 61.8 us (level)
  no operation moved by 1% of the time
where the time goes in v5:
time: 61.8 us; the launch traced here: 61.5 us
  Pallas kernels  60.9 us (99%)
  between operations  0.64 us (1%)
    pallas_call x1, Pallas kernels, fused(): pl.pallas_call(functools.partial(frame_kernel, ntp, ncb), out_shape=(jax....  59.4 us
    pallas_call x1, Pallas kernels, fused(): pl.pallas_call(finish, out_shape=(jax.ShapeDtypeStruct(temporal.shape, bf...  1.5 us

profile of v5, /device:TPU:0, one launch (start us, length us, event | category | flops | bytes accessed | tf_op | source)
XLA Modules:
  0.0 61.5 jit_solution(11365413088667265274)
XLA Ops:
  0.6 59.4 %shard_map.140 = (bf16[32,512]{1,0:T(8,128)(2,1)}, bf16[2,128,128]{2,1,0:T(8,128)(2,1)}) custom-call(bf16[32,512]{1,0:T(8,128)(2,1)} %hid.1, bf16[512]{0:T(512)(128)(2,1)} %gain.1, s32[4]{0:T(128)} %lengths.1, s32[2,128]{1,0:T(2,128)} %bitcast.3, bf16[2,1024]{1,0:T(2,128)(2,1)} %depth_gain.1, bf16[3,4096,512]{2,1,0:T(8,128)(2,1)} %w_qkv.1, ...), custom_call_target="tpu_custom_call" | custom-call | tf_op jit(solution)/shard_map/pallas_call | solution.py:624
  60.0 1.5 %shard_map.141 = (bf16[32,512]{1,0:T(8,128)(2,1)}, bf16[2,128,128]{2,1,0:T(8,128)(2,1)}) custom-call(bf16[32,512]{1,0:T(8,128)(2,1)} %get-tuple-element.4.temporal, bf16[2,128,128]{2,1,0:T(8,128)(2,1)} %get-tuple-element.5.depth), custom_call_target="tpu_custom_call" | custom-call | tf_op jit(solution)/shard_map/pallas_call | solution.py:644

commit v6 on v5

--- a/solution.py
+++ b/solution.py
@@ -350,48 +350,48 @@
 
     scale = 1.0 / math.sqrt(HEAD_DIM)
     slots = per_dev * CACHE
-    row = lax.broadcasted_iota(jnp.int32, (blk, slots), 0)
-    col = lax.broadcasted_iota(jnp.int32, (blk, slots), 1)
-    count = jnp.zeros((blk, slots), jnp.int32)
+    lanes = ntp * blk
+    row = lax.broadcasted_iota(jnp.int32, (lanes, slots), 0)
+    col = lax.broadcasted_iota(jnp.int32, (lanes, slots), 1)
+    count = jnp.zeros((lanes, slots), jnp.int32)
     for r in range(per_dev):
         count = jnp.where(col // CACHE == r, lengths[r], count)
     live = (row % per_dev == col // CACHE) & (col % CACHE < count)
-    head_of = lax.broadcasted_iota(jnp.int32, (blk, HEAD_DIM), 0) // per_dev
-    queries, products = [], []
+    head_of = lax.broadcasted_iota(jnp.int32, (lanes, HEAD_DIM), 0) // per_dev % heads
+    query = qkv_recv[0].reshape(lanes, HEAD_DIM).astype(f32)
+    key_new = qkv_recv[1].reshape(lanes, HEAD_DIM).astype(f32)
+    value_new = qkv_recv[2].reshape(lanes, HEAD_DIM).astype(f32)
+    spread = jnp.concatenate(
+        [jnp.where(head_of == h, query, 0.0) for h in range(heads)], axis=1
+    ).astype(bf16)
+    products = []
     for s in range(ntp):
-        query = qkv_recv[0, s].astype(f32)
-        spread = jnp.concatenate(
-            [jnp.where(head_of == h, query, 0.0) for h in range(heads)], axis=1
-        ).astype(bf16)
-        cols = slice(s * feat, (s + 1) * feat)
-        old_keys = vk[:, :, cols].reshape(slots, feat)
+        old_keys = vk[:, :, s * feat : (s + 1) * feat].reshape(slots, feat)
         products.append(
             lax.dot_general(
-                old_keys, spread, (((1,), (1,)), ((), ())), preferred_element_type=f32
+                old_keys,
+                spread[s * blk : (s + 1) * blk, :],
+                (((1,), (1,)), ((), ())),
+                preferred_element_type=f32,
             )
         )
-        queries.append(query)
-    products = jnp.transpose(jnp.concatenate(products, axis=1))
+    scores = jnp.transpose(jnp.concatenate(products, axis=1)) * scale
+    scores = jnp.where(live, scores, -1e30)
+    fresh = jnp.sum(query * key_new, axis=1, keepdims=True) * scale
+    top = jnp.maximum(jnp.max(scores, axis=1, keepdims=True), fresh)
+    weight = jnp.exp(scores - top)
+    weight_new = jnp.exp(fresh - top)
+    norm = jnp.sum(weight, axis=1, keepdims=True) + weight_new
+    probs = (weight / norm).astype(bf16)
+    mixed_new = (weight_new / norm).astype(bf16).astype(f32) * value_new
     for s in range(ntp):
-        query = queries[s]
-        key_new = qkv_recv[1, s].astype(f32)
-        value_new = qkv_recv[2, s].astype(f32)
-        cols = slice(s * feat, (s + 1) * feat)
-        scores = products[s * blk : (s + 1) * blk, :] * scale
-        scores = jnp.where(live, scores, -1e30)
-        fresh = jnp.sum(query * key_new, axis=1, keepdims=True) * scale
-        top = jnp.maximum(jnp.max(scores, axis=1, keepdims=True), fresh)
-        weight = jnp.exp(scores - top)
-        weight_new = jnp.exp(fresh - top)
-        norm = jnp.sum(weight, axis=1, keepdims=True) + weight_new
-        probs = (weight / norm).astype(bf16)
-        prob_new = (weight_new / norm).astype(bf16).astype(f32)
-        old_values = vv[:, :, cols].reshape(slots, feat)
-        wide = jnp.dot(probs, old_values, preferred_element_type=f32)
-        mixed = prob_new * value_new
+        mine = slice(s * blk, (s + 1) * blk)
+        old_values = vv[:, :, s * feat : (s + 1) * feat].reshape(slots, feat)
+        wide = jnp.dot(probs[mine, :], old_values, preferred_element_type=f32)
+        mixed = mixed_new[mine, :]
         for h in range(heads):
             mixed = mixed + jnp.where(
-                head_of == h, wide[:, h * HEAD_DIM : (h + 1) * HEAD_DIM], 0.0
+                head_of[mine, :] == h, wide[:, h * HEAD_DIM : (h + 1) * HEAD_DIM], 0.0
             )
         att_send[s] = mixed.astype(bf16)
     arriving = [

time: 61.8 us -> 61.8 us (level)
  no operation moved by 1% of the time
where the time goes in v6:
time: 61.8 us; the launch traced here: 61.5 us
  Pallas kernels  60.9 us (99%)
  between operations  0.64 us (1%)
    pallas_call x1, Pallas kernels, fused(): pl.pallas_call(functools.partial(frame_kernel, ntp, ncb), out_shape=(jax....  59.4 us
    pallas_call x1, Pallas kernels, fused(): pl.pallas_call(finish, out_shape=(jax.ShapeDtypeStruct(temporal.shape, bf...  1.5 us

profile of v6, /device:TPU:0, one launch (start us, length us, event | category | flops | bytes accessed | tf_op | source)
XLA Modules:
  0.0 61.5 jit_solution(11815052384448996557)
XLA Ops:
  0.6 59.4 %shard_map.140 = (bf16[32,512]{1,0:T(8,128)(2,1)}, bf16[2,128,128]{2,1,0:T(8,128)(2,1)}) custom-call(bf16[32,512]{1,0:T(8,128)(2,1)} %hid.1, bf16[512]{0:T(512)(128)(2,1)} %gain.1, s32[4]{0:T(128)} %lengths.1, s32[2,128]{1,0:T(2,128)} %bitcast.3, bf16[2,1024]{1,0:T(2,128)(2,1)} %depth_gain.1, bf16[3,4096,512]{2,1,0:T(8,128)(2,1)} %w_qkv.1, ...), custom_call_target="tpu_custom_call" | custom-call | tf_op jit(solution)/shard_map/pallas_call | solution.py:624
  60.0 1.5 %shard_map.141 = (bf16[32,512]{1,0:T(8,128)(2,1)}, bf16[2,128,128]{2,1,0:T(8,128)(2,1)}) custom-call(bf16[32,512]{1,0:T(8,128)(2,1)} %get-tuple-element.4.temporal, bf16[2,128,128]{2,1,0:T(8,128)(2,1)} %get-tuple-element.5.depth), custom_call_target="tpu_custom_call" | custom-call | tf_op jit(solution)/shard_map/pallas_call | solution.py:644
